TPU v7x, 512 devices: a whole 4x8x8 slice. The times are simulated.
512 devices in a mesh: tm: 32 (over z, x), height: 16 (over y, core).
Axes of the slice: x: 4, y: 8, z: 8, core: 2. Of those that a mesh axis runs over, the one named last changes fastest.
Arguments:
- video_latents: bfloat16 [64, 16, 160, 1024], P('tm', 'height'), may hold values from -6 to 6
- qkv_weight: bfloat16 [1024, 3072], P('tm'), may hold values from -0.1875 to 0.1875
- beta_weight: bfloat16 [1024, 8], replicated, may hold values from -0.1875 to 0.1875
- conv_kernel: float32 [3, 3, 3072], replicated, may hold values from -1.75 to 1.75
- decay_rate: float32 [64, 8], P('tm'), may hold values from 0 to 4, as said below
- step_rate: float32 [8], replicated, may hold values from 0.3 to 1.5
- output_gain: float32 [1024], replicated, may hold values from 0.25 to 1.75
Outputs:
- attended: bfloat16 [64, 16, 160, 1024], P('tm', 'height')
Inputs may be any that keep to these rules, and one draw needn't show every extreme that they name: `decay_rate`: positive decay exponents.
All inputs are finite; a program needn't handle non-finite values.
Results may differ from a plain program's by a relative error of at most 0.008.
Values may be sent and summed in bfloat16 or wider, within the bound.
A program may use at most 128 MiB of HBM per device.

v0:
```python
import jax
import jax.numpy as jnp
from jax import lax
from jax.sharding import PartitionSpec as P

epsilon = 1e-06


def with_halo(x, sides, width):
    for axis, dim in sides:
        size, length = (lax.axis_size(axis), x.shape[dim])
        up = [(i, (i + 1) % size) for i in range(size - 1)]
        down = [(j, i) for i, j in up]
        last = lax.slice_in_dim(x, length - width, length, axis=dim)
        initial = lax.slice_in_dim(x, 0, width, axis=dim)
        before = lax.ppermute(last, axis, up)
        after = lax.ppermute(initial, axis, down)
        x = jnp.concatenate([before, x, after], axis=dim)
    return x


def entering(x, axis, combine, identity):
    length, mine = (lax.axis_size(axis), lax.axis_index(axis))
    everything = jax.tree.map(lambda part: lax.all_gather(part, axis), x)
    start = jax.tree.map(
        lambda part, zero: jnp.broadcast_to(jnp.asarray(zero, part.dtype), part.shape), x, identity
    )

    def hop(k, before):
        reached = k < mine
        new = combine(before, jax.tree.map(lambda part: part[k], everything))
        return jax.tree.map(lambda a, b: jnp.where(reached, a, b), new, before)

    return lax.fori_loop(0, length, hop, start)


def mix_stream(extended, kernel):
    count_rows = extended.shape[0] - 2
    count_cols = extended.shape[1]
    padded = jnp.pad(extended.astype(jnp.float32), ((0, 0), (1, 1), (0, 0)))
    summed = jnp.zeros((count_rows, count_cols, extended.shape[2]), jnp.float32)
    for offset_row in range(3):
        for offset_col in range(3):
            summed = (
                summed
                + padded[offset_row : offset_row + count_rows, offset_col : offset_col + count_cols]
                * kernel[offset_row, offset_col]
            )
    return jax.nn.silu(summed)


def normalize(entries):
    return entries * lax.rsqrt(jnp.sum(entries * entries, axis=-1, keepdims=True) + epsilon)


def advance(key_gram, written, decay_row, step_size):
    order_size = key_gram.shape[-1]
    identity = jnp.broadcast_to(jnp.eye(order_size, dtype=jnp.float32), key_gram.shape)
    system = identity + step_size[:, None, None] * key_gram
    factor = jnp.linalg.cholesky(system)
    stacked = jnp.concatenate([identity, step_size[:, None, None] * written], axis=2)
    halfway = lax.linalg.triangular_solve(factor, stacked, left_side=True, lower=True)
    solved = lax.linalg.triangular_solve(
        factor, halfway, left_side=True, lower=True, transpose_a=True
    )
    retain = jnp.exp(-decay_row)[:, None, None]
    return (retain * solved[:, :, :order_size], retain * solved[:, :, order_size:])


def apply_map(matrix, state):
    return jnp.einsum("hij,hjk->hik", matrix, state, precision=lax.Precision.HIGHEST)


def compose(earlier, latter):
    product = apply_map(latter[0], earlier[0])
    shifted = apply_map(latter[0], earlier[1]) + latter[1]
    return (product, shifted)


def body(video_latents, qkv_weight, beta_weight, conv_kernel, decay_rate, step_rate, output_gain):
    frame_count, count_rows, count_cols, model_width = video_latents.shape
    head_count = beta_weight.shape[1]
    head_size = model_width // head_count
    full_weight = lax.all_gather(qkv_weight, "tm", axis=0, tiled=True)
    projected = (
        jnp.dot(
            video_latents.reshape(-1, model_width), full_weight, preferred_element_type=jnp.float32
        )
        .astype(jnp.bfloat16)
        .reshape(frame_count, count_rows, count_cols, 3 * model_width)
    )
    extended = with_halo(projected, (("height", 1),), 1)
    conv_frames = jax.vmap(mix_stream, in_axes=(0, None))
    streams = [
        conv_frames(
            extended[..., stream * model_width : (stream + 1) * model_width],
            conv_kernel[:, :, stream * model_width : (stream + 1) * model_width],
        ).reshape(frame_count, -1, head_count, head_size)
        for stream in range(3)
    ]
    queries = normalize(streams[0]).astype(jnp.bfloat16)
    keys_unit = normalize(streams[1]).astype(jnp.bfloat16)
    values_b = streams[2].astype(jnp.bfloat16)
    beta_gates = jax.nn.sigmoid(
        jnp.dot(
            video_latents.reshape(frame_count, -1, model_width),
            beta_weight,
            preferred_element_type=jnp.float32,
        )
    )
    weighted = (beta_gates[..., None] * keys_unit.astype(jnp.float32)).astype(jnp.bfloat16)
    key_gram = jnp.einsum(
        "fthi,fthj->fhij", weighted, keys_unit, preferred_element_type=jnp.float32
    )
    written = jnp.einsum("fthi,fthj->fhij", weighted, values_b, preferred_element_type=jnp.float32)
    height_count = lax.axis_size("height")
    key_gram, written = lax.psum((key_gram, written), "height")
    total_tokens = frame_count * lax.axis_size("tm") * count_rows * height_count * count_cols
    step_size = step_rate * (head_size / total_tokens)
    transition, source = jax.vmap(advance, in_axes=(0, 0, 0, None))(
        key_gram, written, decay_rate, step_size
    )
    composed = (transition[0], source[0])
    frame = 1
    composed = compose(composed, (transition[frame], source[frame]))
    identity = jnp.broadcast_to(jnp.eye(head_size, dtype=jnp.float32), composed[0].shape)
    prefix = entering(composed, "tm", compose, (identity, jnp.zeros_like(composed[1])))
    incoming = prefix[1]
    states = []
    state = incoming
    for frame in range(frame_count):
        state = apply_map(transition[frame], state) + source[frame]
        states.append(state)
    carried_b = jnp.stack(states, axis=0).astype(jnp.bfloat16)
    readout = jnp.einsum("fthi,fhij->fthj", queries, carried_b, preferred_element_type=jnp.float32)
    head_gain = output_gain.reshape(head_count, head_size)
    scaled = (
        readout
        * lax.rsqrt(jnp.mean(readout * readout, axis=-1, keepdims=True) + epsilon)
        * head_gain
    )
    return scaled.astype(jnp.bfloat16).reshape(frame_count, count_rows, count_cols, model_width)


def solution(mesh):
    placed = (P("tm", "height", None, None), P("tm", None), P(), P(), P("tm", None), P(), P())
    return jax.shard_map(
        body, mesh=mesh, in_specs=placed, out_specs=P("tm", "height", None, None), check_vma=False
    )
```

profile of v0, /device:TPU:1, one launch (start us, length us, event | category | flops | bytes accessed | tf_op | source)
XLA Modules:
  0.0 1009.4 jit_solution(7067609325366823950)
XLA Ops:
  7.3 103.1 %all-gather.6.cloned.1.call-done = bf16[1024,3072]{1,0:T(8,128)(2,1)} async-done(((bf16[32,3072]{1,0:T(8,128)(2,1)}), bf16[1024,3072]{1,0:T(8,128)(2,1)}) %all-gather.6.cloned.1.call-update) | async-done | bytes 6291472 | tf_op jit(solution)/shard_map/all_gather | solution.py:84
  110.5 5.0 convolution_convert_fusion
  115.5 4.0 collective-permute-start
  119.5 1.9 collective-permute-start.1
  122.0 19.1 %collective-permute-done = bf16[2,1,160,3072]{3,2,0,1:T(8,128)(2,1)} collective-permute-done((bf16[2,1,160,3072]{3,2,0,1:T(8,128)(2,1)S(1)}, bf16[2,1,160,3072]{3,2,0,1:T(8,128)(2,1)}, u32[]{:S(2)}, u32[]{:S(2)}) %collective-permute-start) | collective-permute-done | bytes 1966112 | tf_op jit(solution)/shard_map/ppermute | solution.py:16
  141.0 4.5 collective-permute-done.1
  145.5 3.1 pad_maximum_fusion
  148.6 4.4 slice_convert_fusion.1
  155.4 6.2 multiply_convert_fusion.1
  166.3 116.0 %all-reduce.6.cloned.1.call-done = (f32[2,8,128,128]{2,3,1,0:T(8,128)}, f32[2,8,128,128]{2,3,1,0:T(8,128)}) async-done(((f32[2,8,128,128]{2,3,1,0:T(8,128)}, f32[2,8,128,128]{2,3,1,0:T(8,128)}), (f32[2,8,128,128]{2,3,1,0:T(8,128)}, f32[2,8,128,128]{2,3,1,0:T(8,128)})) %all-reduce.6.cloned.1.call-update) | async-done | bytes 2097168 | tf_op jit(solution)/shard_map/psum | solution.py:117
  285.4 2.3 fusion.66
  287.7 188.3 %custom-call.9 = f32[2,8,128,128]{3,2,1,0:T(8,128)S(1)} custom-call(f32[2,8,128,128]{3,2,1,0:T(8,128)} %fusion.66), custom_call_target="Cholesky" | custom-call | tf_op jit(solution)/shard_map/vmap(jit(cholesky))/cholesky | solution.py:60
  477.4 158.0 %custom-call.10 = f32[2,8,1,128,128]{3,4,2,1,0:T(8,128)S(1)} custom-call(f32[2,8,1,128,128]{4,3,2,1,0:T(8,128)} %select_bitcast_fusion), custom_call_target="InvertDiagBlocksLowerTriangular" | custom-call | tf_op jit(solution)/shard_map/vmap()/triangular_solve | solution.py:63
  635.5 2.0 fusion.8
  637.5 1.9 fusion.63
  643.9 6.4 divide_multiply_fusion
  652.5 137.1 %all-gather.10.cloned.1.call-done = f32[256,128,128]{2,1,0:T(8,128)} async-done(((f32[8,128,128]{2,1,0:T(8,128)}), f32[256,128,128]{2,1,0:T(8,128)}) %all-gather.10.cloned.1.call-update) | async-done | bytes 16777232 | tf_op jit(solution)/shard_map/all_gather | solution.py:24
  789.6 146.4 %all-gather.8.cloned.1.call-done = f32[256,128,128]{2,1,0:T(8,128)} async-done(((f32[8,128,128]{2,1,0:T(8,128)}), f32[256,128,128]{2,1,0:T(8,128)}) %all-gather.8.cloned.1.call-update) | async-done | bytes 16777232 | tf_op jit(solution)/shard_map/all_gather | solution.py:24
  936.1 62.4 %while.14 = (s32[]{:T(128)}, f32[8,128,128]{2,1,0:T(8,128)S(1)}, s32[]{:T(128)}, f32[32,8,128,128]{3,2,1,0:T(8,128)}, f32[32,8,128,128]{3,2,1,0:T(8,128)}, /*index=5*/s32[]{:T(128)}, s32[]{:T(128)}) while((s32[]{:T(128)}, f32[8,128,128]{2,1,0:T(8,128)S(1)}, s32[]{:T(128)}, f32[32,8,128,128]{3,2,1,0:T(8,128)}, ...), condition=%wide.region_6.7_spmd.clone, body=%wide.region_5.6_spmd.clone.sunk | while | flops 201850880 | bytes 3672671 | solution.py:34
  936.1 2.0 fusion.96
  938.1 1.9 fusion.96
  942.0 1.9 fusion.96
  965.4 1.9 fusion.96
  982.9 1.9 fusion.96
  (131 shorter events, 75.4 us)
Async XLA Ops:
  6.5 103.9 %copy-start = (bf16[2,1,160,1024]{3,2,1,0:T(8,128)(2,1)S(1)}, bf16[2,1,160,1024]{3,2,1,0:T(8,128)(2,1)}, u32[]{:S(2)}) copy-start(bf16[2,1,160,1024]{3,2,1,0:T(8,128)(2,1)} %param.9) | copy-start | bytes 1966084
  6.5 103.9 %all-gather.6.cloned.1.call-start = ((), (), s32[]{:S(2)}) async-start(), calls=%async_computation | async-start | bytes 6488064 | tf_op jit(solution)/shard_map/all_gather | solution.py:84
  7.3 275.0 %all-reduce.6.cloned.1.call-start = ((), (), s32[]{:S(2)}) async-start(), calls=%async_computation.3 | async-start | bytes 4194304 | tf_op jit(solution)/shard_map/psum | solution.py:117
  110.5 10.9 %copy-start.6 = (bf16[1024,8]{0,1:T(8,128)(2,1)S(1)}, bf16[1024,8]{0,1:T(8,128)(2,1)}, u32[]{:S(2)}) copy-start(bf16[1024,8]{0,1:T(8,128)(2,1)} %param.11) | copy-start | bytes 49156
  110.5 11.4 %copy-start.5 = (f32[3,3,3072]{2,1,0:T(4,128)S(1)}, f32[3,3,3072]{2,1,0:T(4,128)}, u32[]{:S(2)}) copy-start(f32[3,3,3072]{2,1,0:T(4,128)} %param.12) | copy-start | bytes 331780
  115.5 25.5 %collective-permute-start = (bf16[2,1,160,3072]{3,2,0,1:T(8,128)(2,1)S(1)}, bf16[2,1,160,3072]{3,2,0,1:T(8,128)(2,1)}, u32[]{:S(2)}, u32[]{:S(2)}) collective-permute-start(bf16[2,1,160,3072]{3,2,0,1:T(8,128)(2,1)S(1)} %bitcast.135), channel_id=1, source_target_pairs={{0,1},{1,2},{2,3},{3,4},{4,5},{5,6},{6,7},{7,8},{8,9},{9,10},{10,1... | collective-permute-start | bytes 5898248 | tf_op jit(solution)/shard_map/ppermute | solution.py:16
  119.5 26.1 %collective-permute-start.1 = (bf16[2,1,160,3072]{3,2,0,1:T(8,128)(2,1)S(1)}, bf16[2,1,160,3072]{3,2,0,1:T(8,128)(2,1)}, u32[]{:S(2)}, u32[]{:S(2)}) collective-permute-start(bf16[2,1,160,3072]{3,2,0,1:T(8,128)(2,1)S(1)} %bitcast.136), channel_id=1, source_target_pairs={{1,0},{2,1},{3,2},{4,3},{5,4},{6,5},{7,6},{8,7},{9,8},{10,9},{11,1... | collective-permute-start | bytes 5898248 | tf_op jit(solution)/shard_map/ppermute | solution.py:17
  165.6 0.7 copy-start.9
  165.6 0.7 copy-start.8
  165.6 624.0 %all-gather.10.cloned.1.call-start = ((), (), s32[]{:S(2)}) async-start(), calls=%async_computation.2 | async-start | bytes 17301504 | tf_op jit(solution)/shard_map/all_gather | solution.py:24
  639.7 1.0 copy-start.2
  642.1 293.9 %all-gather.8.cloned.1.call-start = ((), (), s32[]{:S(2)}) async-start(), calls=%async_computation.1 | async-start | bytes 17301504 | tf_op jit(solution)/shard_map/all_gather | solution.py:24
  936.0 62.4 %copy-start.3 = (f32[2,8,128,128]{3,2,1,0:T(8,128)S(1)}, f32[2,8,128,128]{3,2,1,0:T(8,128)}, u32[]{:S(2)}) copy-start(f32[2,8,128,128]{3,2,1,0:T(8,128)} %copy-done.2) | copy-start | bytes 3145732
  999.1 1.1 copy-start.4
  1000.2 0.8 copy-start.7
  1001.1 1.8 copy-start.1
Sparse Core Ops, SparseCore 0:
  10.5 99.8 all-gather.5
  165.7 116.5 all-reduce.5
  642.2 147.3 all-gather.9
  792.6 143.3 all-gather.7
where the time goes:
time: 1010 us
  waiting for transfers between devices  527 us (52%)
  other arithmetic  377 us (37%)
  matrix products  77.2 us (8%)
  between operations  13.5 us (1%)
    all_gather x2, waiting for transfers between devices, entering(): everything = jax.tree.map(lambda part: lax.all_gather(part, axis), x)  284 us
    another operation x4, other arithmetic, advance(): factor = jnp.linalg.cholesky(system)  189 us
    another operation x3, other arithmetic, advance(): lax.linalg.triangular_solve(factor, halfway, left_side=True, lower=True,...  159 us
    psum x1, waiting for transfers between devices, body(): key_gram, written = lax.psum((key_gram, written), 'height')  116 us
    all_gather x1, waiting for transfers between devices, body(): full_weight = lax.all_gather(qkv_weight, 'tm', axis=0, tiled=True)  103 us
    dot_general x36, matrix products, apply_map(): jnp.einsum('hij,hjk->hik', matrix, state, precision=lax.Precision.HIGHEST)  64.3 us
  transfers between devices with their start and end apart: 6, of which 6 were waited for; matrix products, arithmetic and copies ran while one was open for 1% of the time, Pallas kernels for 0%

commit v1 on v0

v1 whole, which is shorter than its diff:
```python
import functools

import jax
import jax.numpy as jnp
from jax import lax
from jax.experimental import pallas as pl
from jax.experimental.pallas import tpu as pltpu
from jax.sharding import PartitionSpec as P

MESH = pl.DeviceIdType.MESH
EPS = 1e-06
F32 = jnp.float32
BF16 = jnp.bfloat16
NX, NZ, NY = 4, 8, 8
TOKENS = 64 * 16 * 160
DK = 128
VM = pl.BlockSpec(memory_space=pltpu.VMEM)
SM = pl.BlockSpec(memory_space=pltpu.SMEM)
ANY = pl.BlockSpec(memory_space=pl.ANY)


def place():
    t, h = lax.axis_index("tm"), lax.axis_index("height")
    return lax.rem(t, NX), lax.div(h, 2), lax.div(t, NX), lax.rem(h, 2)


def dev(x, y, z, c):
    return (z * NX + x, y * 2 + c)


def up(i, d, n):
    return lax.rem(i + d, n)


def down(i, d, n):
    return lax.rem(i + n - d, n)


def rcopy(src, dst, ssem, rsem, to):
    return pltpu.make_async_remote_copy(
        src_ref=src, dst_ref=dst, send_sem=ssem, recv_sem=rsem, device_id=to, device_id_type=MESH
    )


def signal(barrier, to):
    pl.semaphore_signal(barrier, inc=1, device_id=to, device_id_type=MESH)


def mix_kernel(
    x_ref, w_ref, bw_ref, ck_ref, q_ref, g_ref,
    xe, wg, proj, kv, wt, beta, qbuf, part, got,
    s_halo, r_halo, s_ax, r_ax, s_az, r_az, s_bz, r_bz, s_bx, r_bx, s_g, r_g, s_q, r_q, l_q,
):
    x, y, z, c = place()
    xe[:, 1 + c] = x_ref[...]
    for s in range(4):
        for g in range(3):
            col = pl.multiple_of(g * 1024 + c * 512 + s * 128, 128)
            wg[s, z, x, :, g * 128 : (g + 1) * 128] = w_ref[:, pl.ds(col, 128)]

    barrier = pltpu.get_barrier_semaphore()
    signal(barrier, dev(x, y, up(z, 1, NZ), c))
    signal(barrier, dev(x, y, down(z, 1, NZ), c))
    for d in range(1, NX):
        signal(barrier, dev(up(x, d, NX), y, z, c))
    for d in range(1, NY):
        signal(barrier, dev(x, up(y, d, NY), z, c))
    signal(barrier, dev(x, up(y, 1, NY), z, 1 - c))
    signal(barrier, dev(x, down(y, 1, NY), z, 1 - c))
    signal(barrier, dev(x, y, z, 1 - c))
    pl.semaphore_wait(barrier, 15)

    ax = []
    for d in range(1, NX):
        own = wg.at[pl.ds(0, 2), z, x]
        ax.append(rcopy(own, own, s_ax.at[d - 1], r_ax.at[d - 1], dev(up(x, d, NX), y, z, c)))
        ax[-1].start()

    def ax_wait():
        for d in range(1, NX):
            src = wg.at[pl.ds(0, 2), z, down(x, d, NX)]
            rcopy(src, src, s_ax.at[d - 1], r_ax.at[d - 1], dev(x, y, z, 1 - c)).wait_recv()
        for cp in ax:
            cp.wait_send()

    zs = (dev(x, y, up(z, 1, NZ), c), dev(x, y, down(z, 1, NZ), c))

    def zblock(view, dr, k):
        zz = down(z, k, NZ) if dr == 0 else up(z, k, NZ)
        return view(zz, dr if k == 4 else None)

    def zring_send(view, ssem, rsem, k):
        for dr in range(2):
            zz = down(z, k - 1, NZ) if dr == 0 else up(z, k - 1, NZ)
            ref = view(zz, dr if k == 4 else None)
            rcopy(ref, ref, ssem.at[dr, k - 1], rsem.at[dr, k - 1], zs[dr]).start()

    def zring_recv(view, ssem, rsem, k):
        for dr in range(2):
            ref = zblock(view, dr, k)
            rcopy(ref, ref, ssem.at[dr, k - 1], rsem.at[dr, k - 1], zs[dr]).wait_recv()

    def zring_done(view, ssem, rsem):
        for k in range(1, 5):
            for dr in range(2):
                ref = zblock(view, dr, k)
                rcopy(ref, ref, ssem.at[dr, k - 1], rsem.at[dr, k - 1], zs[dr]).wait_send()

    def view_b(zz, half):
        if half is None:
            return wg.at[pl.ds(2, 2), zz, x]
        return wg.at[pl.ds(2 + half, 1), zz, x]

    def view_a(a):
        def view(zz, half):
            if half is None:
                return wg.at[a, zz]
            return wg.at[a, zz, pl.ds(2 * half, 2)]

        return view

    va = [view_a(0), view_a(1)]
    xs = (dev(up(x, 1, NX), y, z, c), dev(down(x, 1, NX), y, z, c))

    def bx_block(b, dr, k):
        xx = down(x, k, NX) if dr == 0 else up(x, k, NX)
        if k == 2:
            return wg.at[b, pl.ds(4 * dr, 4), xx]
        return wg.at[b, :, xx]

    def bx_send(i, k):
        for dr in range(2):
            xx = x if k == 1 else (down(x, 1, NX) if dr == 0 else up(x, 1, NX))
            ref = wg.at[2 + i, :, xx] if k == 1 else wg.at[2 + i, pl.ds(4 * dr, 4), xx]
            rcopy(ref, ref, s_bx.at[i, dr, k - 1], r_bx.at[i, dr, k - 1], xs[dr]).start()

    def bx_recv(i, k):
        for dr in range(2):
            ref = bx_block(2 + i, dr, k)
            rcopy(ref, ref, s_bx.at[i, dr, k - 1], r_bx.at[i, dr, k - 1], xs[dr]).wait_recv()

    def bx_done(i):
        for k in (1, 2):
            for dr in range(2):
                ref = bx_block(2 + i, dr, k)
                rcopy(ref, ref, s_bx.at[i, dr, k - 1], r_bx.at[i, dr, k - 1], xs[dr]).wait_send()

    zring_send(view_b, s_bz, r_bz, 1)

    mine = xe.at[:, 1 + c]
    theirs = xe.at[:, 2 - c]
    rcopy(mine, mine, s_halo.at[0], r_halo.at[0], dev(x, y, z, 1 - c)).start()
    for e in range(2):

        @pl.when((c == 1) & (y < NY - 1))
        def _():
            rcopy(mine, xe.at[:, 0], s_halo.at[1 + e], r_halo.at[1], dev(x, up(y, 1, NY), z, e)).start()

        @pl.when((c == 0) & (y > 0))
        def _():
            rcopy(mine, xe.at[:, 3], s_halo.at[1 + e], r_halo.at[2], dev(x, down(y, 1, NY), z, e)).start()

    @pl.when(y == 0)
    def _():
        xe[:, 0] = jnp.zeros((2, 160, 1024), BF16)

    @pl.when(y == NY - 1)
    def _():
        xe[:, 3] = jnp.zeros((2, 160, 1024), BF16)

    ax_wait()
    zring_send(va[0], s_az.at[0], r_az.at[0], 1)
    for k in (1, 2, 3):
        zring_recv(view_b, s_bz, r_bz, k)
        zring_send(view_b, s_bz, r_bz, k + 1)
        zring_recv(va[0], s_az.at[0], r_az.at[0], k)
        zring_send(va[0], s_az.at[0], r_az.at[0], k + 1)
    zring_recv(view_b, s_bz, r_bz, 4)
    bx_send(0, 1)
    zring_send(va[1], s_az.at[1], r_az.at[1], 1)

    rcopy(theirs, theirs, s_halo.at[0], r_halo.at[0], dev(x, y, z, 1 - c)).wait_recv()

    @pl.when(y > 0)
    def _():
        rcopy(mine, xe.at[:, 0], s_halo.at[1], r_halo.at[1], dev(x, y, z, 1 - c)).wait_recv()

    @pl.when(y < NY - 1)
    def _():
        rcopy(mine, xe.at[:, 3], s_halo.at[1], r_halo.at[2], dev(x, y, z, 1 - c)).wait_recv()

    for f in range(2):
        logits = jnp.dot(xe[f, 1:3].reshape(320, 1024), bw_ref[...], preferred_element_type=F32)
        gates = jax.nn.sigmoid(logits)
        gates = jnp.where(c == 0, gates[:, 0:4], gates[:, 4:8])
        for s in range(4):
            beta[f, s] = jnp.broadcast_to(gates[:, s : s + 1], (320, 128))

    def step(i, carry):
        pair, f = lax.div(i, 2), lax.rem(i, 2)
        slot = lax.rem(pair, 2) * 2 + lax.div(pair, 2)

        @pl.when(i == 0)
        def _():
            zring_recv(va[0], s_az.at[0], r_az.at[0], 4)

        @pl.when(i == 1)
        def _():
            bx_recv(0, 1)
            bx_send(0, 2)
            bx_send(1, 1)
            zring_recv(va[1], s_az.at[1], r_az.at[1], 1)
            zring_send(va[1], s_az.at[1], r_az.at[1], 2)

        @pl.when(i == 2)
        def _():
            bx_recv(0, 2)
            zring_recv(va[1], s_az.at[1], r_az.at[1], 2)
            zring_send(va[1], s_az.at[1], r_az.at[1], 3)

        @pl.when(i == 3)
        def _():
            bx_recv(1, 1)
            bx_send(1, 2)
            zring_recv(va[1], s_az.at[1], r_az.at[1], 3)
            zring_send(va[1], s_az.at[1], r_az.at[1], 4)

        @pl.when(i == 4)
        def _():
            zring_recv(va[1], s_az.at[1], r_az.at[1], 4)

        @pl.when(i == 6)
        def _():
            bx_recv(1, 2)

        proj[...] = (
            jnp.dot(
                xe[f].reshape(640, 1024), wg[slot].reshape(1024, 384), preferred_element_type=F32
            )
            .astype(BF16)
            .reshape(4, 160, 384)
        )
        ids = lax.broadcasted_iota(jnp.int32, (160, 128), 0)
        for g in range(3):
            col = pl.multiple_of(g * 1024 + (4 * c + slot) * 128, 128)
            taps = [[ck_ref[a, pl.ds(b, 1), pl.ds(col, 128)] for b in range(3)] for a in range(3)]
            for o in range(2):
                rows = [proj[o + a, :, g * 128 : (g + 1) * 128].astype(F32) for a in range(3)]
                sums = [sum(rows[a] * taps[a][b] for a in range(3)) for b in range(3)]
                total = (
                    jnp.where(ids > 0, pltpu.roll(sums[0], 1, 0), 0.0)
                    + sums[1]
                    + jnp.where(ids < 159, pltpu.roll(sums[2], 159, 0), 0.0)
                )
                s = total * jax.nn.sigmoid(total)
                if g < 2:
                    s = s * lax.rsqrt(jnp.sum(s * s, axis=-1, keepdims=True) + EPS)
                s = s.astype(BF16)
                if g == 0:
                    qbuf[slot, o, f] = s
                else:
                    kv[o * 160 : (o + 1) * 160, (g - 1) * 128 : g * 128] = s
                if g == 1:
                    wt[o * 160 : (o + 1) * 160, :] = (
                        beta[f, slot, o * 160 : (o + 1) * 160, :] * s.astype(F32)
                    ).astype(BF16)
        unit = 2 * slot + f
        part[unit] = lax.dot_general(
            wt[...], kv[...], (((0,), (0,)), ((), ())), preferred_element_type=F32
        ).astype(BF16)

        @pl.when(unit != y)
        def _():
            rcopy(part.at[unit], got.at[y], s_g.at[unit], r_g.at[y], dev(x, unit, z, c)).start()

        @pl.when(f == 1)
        def _():
            rcopy(
                qbuf.at[slot, 1 - c], q_ref.at[4 * c + slot], s_q.at[slot], r_q.at[slot], dev(x, y, z, 1 - c)
            ).start()
            pltpu.make_async_copy(qbuf.at[slot, c], q_ref.at[4 * c + slot], l_q.at[slot]).start()

        return carry

    lax.fori_loop(0, 8, step, 0)

    total = part[y].astype(F32)
    for d in range(1, NY):
        yy = up(y, d, NY)
        rcopy(got.at[yy], got.at[yy], s_g.at[0], r_g.at[yy], dev(x, y, z, 1 - c)).wait_recv()
        total = total + got[yy].astype(F32)
    g_ref[...] = total

    for s in range(4):
        dst = q_ref.at[4 * (1 - c) + s]
        cp = rcopy(qbuf.at[s, 1 - c], dst, s_q.at[s], r_q.at[s], dev(x, y, z, 1 - c))
        cp.wait_recv()
        cp.wait_send()
        pltpu.make_async_copy(qbuf.at[s, c], q_ref.at[4 * c + s], l_q.at[s]).wait()
    for u in range(8):

        @pl.when(u != y)
        def _():
            rcopy(part.at[u], got.at[y], s_g.at[u], r_g.at[y], dev(x, y, z, 1 - c)).wait_send()

    zring_done(view_b, s_bz, r_bz)
    for a in range(2):
        zring_done(va[a], s_az.at[a], r_az.at[a])
        bx_done(a)
    rcopy(mine, mine, s_halo.at[0], r_halo.at[0], dev(x, y, z, 1 - c)).wait_send()
    for e in range(2):

        @pl.when(((c == 1) & (y < NY - 1)) | ((c == 0) & (y > 0)))
        def _():
            rcopy(mine, mine, s_halo.at[1 + e], r_halo.at[1], dev(x, y, z, 1 - c)).wait_send()


def mix(latents, weight, beta_weight, conv_kernel):
    sem = pltpu.SemaphoreType.DMA
    return pl.pallas_call(
        mix_kernel,
        out_shape=(
            jax.ShapeDtypeStruct((8, 2, 160, 128), BF16),
            jax.ShapeDtypeStruct((128, 256), F32),
        ),
        in_specs=[VM] * 4,
        out_specs=(ANY, VM),
        scratch_shapes=[
            pltpu.VMEM((2, 4, 160, 1024), BF16),
            pltpu.VMEM((4, NZ, NX, 32, 384), BF16),
            pltpu.VMEM((4, 160, 384), BF16),
            pltpu.VMEM((320, 256), BF16),
            pltpu.VMEM((320, 128), BF16),
            pltpu.VMEM((2, 4, 320, 128), F32),
            pltpu.VMEM((4, 2, 2, 160, 128), BF16),
            pltpu.VMEM((8, 128, 256), BF16),
            pltpu.VMEM((8, 128, 256), BF16),
            sem((3,)), sem((3,)),
            sem((3,)), sem((3,)),
            sem((2, 2, 4)), sem((2, 2, 4)),
            sem((2, 4)), sem((2, 4)),
            sem((2, 2, 2)), sem((2, 2, 2)),
            sem((8,)), sem((8,)),
            sem((4,)), sem((4,)), sem((4,)),
        ],
        compiler_params=pltpu.CompilerParams(
            collective_id=0, has_side_effects=True, vmem_limit_bytes=40 * 2**20
        ),
        name="mix",
    )(latents, weight, beta_weight, conv_kernel)


def exact(a, b):
    return jnp.dot(a, b, preferred_element_type=F32, precision=lax.Precision.HIGHEST)


def inverse(system):
    ident = (
        lax.broadcasted_iota(jnp.int32, (DK, DK), 0) == lax.broadcasted_iota(jnp.int32, (DK, DK), 1)
    ).astype(F32)
    power = ident - 0.4 * system
    total = ident + power
    for _ in range(4):
        power = exact(power, power)
        total = total + exact(total, power)
    return 0.4 * total


def chain_kernel(
    g_ref, rate_ref, decay_ref, st_ref,
    own, fin, px, zmap, zin, ein, cb, st,
    s_f, r_f, s_x, r_x, s_z, r_z, s_e, r_e, s_st, r_st, s_sib, r_sib, l_st,
):
    x, y, z, c = place()
    f, head = lax.rem(y, 2), 4 * c + lax.div(y, 2)
    barrier = pltpu.get_barrier_semaphore()
    for d in range(1, NX):
        signal(barrier, dev(up(x, d, NX), y, z, c))
    for d in range(1, NY):
        signal(barrier, dev(x, up(y, d, NY), z, c))
    for d in range(1, NZ):
        signal(barrier, dev(x, y, up(z, d, NZ), c))
    signal(barrier, dev(x, y, z, 1 - c))

    step_size = rate_ref[head] * (DK / TOKENS)
    retain = jnp.exp(-jnp.full((DK, DK), decay_ref[f, head], F32))
    gram, written = g_ref[:, :DK], g_ref[:, DK:]
    diagonal = lax.broadcasted_iota(jnp.int32, (DK, DK), 0) == lax.broadcasted_iota(
        jnp.int32, (DK, DK), 1
    )
    system = jnp.where(diagonal, 1.0, 0.0) + (0.5 * step_size) * (gram + gram.T)
    solved = inverse(system)
    transition = retain * solved
    source = retain * exact(solved, step_size * written)
    own[:, :DK] = transition.astype(BF16)
    own[:, DK:] = source.astype(BF16)

    def compose(latter, earlier):
        both = jnp.dot(latter[:, :DK], earlier, preferred_element_type=F32)
        return jnp.concatenate([both[:, :DK], both[:, DK:] + latter[:, DK:].astype(F32)], axis=1).astype(BF16)

    pl.semaphore_wait(barrier, 18)

    pair = rcopy(own, fin, s_f, r_f, dev(x, y + 1 - 2 * f, z, c))
    pair.start()
    pair.wait_recv()
    mine, other = own[...], fin[...]
    both = compose(jnp.where(f == 0, other, mine), jnp.where(f == 0, mine, other))
    px[x] = both
    for d in range(1, NX):
        rcopy(px.at[x], px.at[x], s_x.at[d - 1], r_x.at[d - 1], dev(up(x, d, NX), y, z, c)).start()
    for d in range(1, NX):
        src = px.at[down(x, d, NX)]
        rcopy(src, src, s_x.at[d - 1], r_x.at[d - 1], dev(x, y, z, 1 - c)).wait_recv()
    first = compose(px[1], px[0])
    zmap[0] = compose(compose(px[3], px[2]), first)
    odd, late, last = lax.rem(z, 2) == 1, lax.rem(z, 4) >= 2, z >= 4

    @pl.when(jnp.logical_not(odd))
    def _():
        rcopy(zmap.at[0], zin.at[0], s_z.at[0], r_z.at[0], dev(x, y, z + 1, c)).start()

    third = compose(px[2], first)
    current = jnp.where(f == 0, mine, both)
    before = jnp.where(x == 1, px[0], jnp.where(x == 2, first, third))
    before = compose(current, before)
    own_map = jnp.where(x == 0, current, before)

    fin2 = zmap.at[2]
    fin2[...] = own_map

    @pl.when(odd)
    def _():
        rcopy(zmap.at[0], zin.at[0], s_z.at[0], r_z.at[0], dev(x, y, z, 1 - c)).wait_recv()
        zmap[1] = compose(zmap[0], zin[0])

    @pl.when(jnp.logical_not(odd))
    def _():
        zmap[1] = zmap[0]

    sends2 = lax.rem(z, 4) == 1
    for e in range(2):

        @pl.when(sends2)
        def _():
            rcopy(zmap.at[1], zin.at[1], s_z.at[1 + e], r_z.at[1], dev(x, y, z + 1 + e, c)).start()

    @pl.when(odd)
    def _():
        fin2[...] = compose(fin2[...], zin[0])

    @pl.when(late)
    def _():
        rcopy(zmap.at[1], zin.at[1], s_z.at[1], r_z.at[1], dev(x, y, z, 1 - c)).wait_recv()

    @pl.when(z == 3)
    def _():
        ein[0] = compose(zmap[1], zin[1])[:, DK:]
        for e in range(4):
            rcopy(ein.at[0], ein.at[1], s_e.at[e], r_e, dev(x, y, 4 + e, c)).start()

    @pl.when(late)
    def _():
        fin2[...] = compose(fin2[...], zin[1])

    @pl.when(last)
    def _():
        rcopy(ein.at[0], ein.at[1], s_e.at[0], r_e, dev(x, y, z, 1 - c)).wait_recv()
        m = fin2[...]
        cb[...] = (
            jnp.dot(m[:, :DK], ein[1], preferred_element_type=F32) + m[:, DK:].astype(F32)
        ).astype(BF16)

    @pl.when(jnp.logical_not(last))
    def _():
        cb[...] = fin2[:, DK:]

    st[c, y] = cb[...]
    rcopy(st.at[c, y], st.at[c, y], s_sib.at[y], r_sib.at[y], dev(x, y, z, 1 - c)).start()
    for d in range(1, NY):
        rcopy(cb, st.at[c, y], s_st.at[d - 1], r_st.at[d - 1], dev(x, up(y, d, NY), z, c)).start()
    for d in (1, 7, 2, 6, 3, 5, 4):
        yy = down(y, d, NY)
        rcopy(cb, st.at[c, yy], s_st.at[d - 1], r_st.at[d - 1], dev(x, y, z, 1 - c)).wait_recv()
        rcopy(st.at[c, yy], st.at[c, yy], s_sib.at[yy], r_sib.at[yy], dev(x, y, z, 1 - c)).start()
    mine_out = pltpu.make_async_copy(st.at[c], st_ref.at[c], l_st.at[0])
    mine_out.start()
    for k in range(NY):
        rcopy(st.at[1 - c, k], st.at[1 - c, k], s_sib.at[k], r_sib.at[k], dev(x, y, z, 1 - c)).wait_recv()
    other_out = pltpu.make_async_copy(st.at[1 - c], st_ref.at[1 - c], l_st.at[1])
    other_out.start()

    pair.wait_send()
    for d in range(1, NX):
        rcopy(px.at[x], px.at[x], s_x.at[d - 1], r_x.at[d - 1], dev(x, y, z, 1 - c)).wait_send()

    @pl.when(jnp.logical_not(odd))
    def _():
        rcopy(zmap.at[0], zin.at[0], s_z.at[0], r_z.at[0], dev(x, y, z, 1 - c)).wait_send()

    for e in range(2):

        @pl.when(sends2)
        def _():
            rcopy(zmap.at[1], zin.at[1], s_z.at[1 + e], r_z.at[1], dev(x, y, z, 1 - c)).wait_send()

    @pl.when(z == 3)
    def _():
        for e in range(4):
            rcopy(ein.at[0], ein.at[1], s_e.at[e], r_e, dev(x, y, z, 1 - c)).wait_send()

    for d in range(1, NY):
        rcopy(cb, st.at[c, y], s_st.at[d - 1], r_st.at[d - 1], dev(x, y, z, 1 - c)).wait_send()
    for k in range(NY):
        rcopy(st.at[c, k], st.at[c, k], s_sib.at[k], r_sib.at[k], dev(x, y, z, 1 - c)).wait_send()
    mine_out.wait()
    other_out.wait()


def chain(gram, step_rate, decay_rate):
    sem = pltpu.SemaphoreType.DMA
    return pl.pallas_call(
        chain_kernel,
        out_shape=jax.ShapeDtypeStruct((2, NY, DK, DK), BF16),
        in_specs=[VM, SM, SM],
        out_specs=ANY,
        scratch_shapes=[
            pltpu.VMEM((DK, 2 * DK), BF16),
            pltpu.VMEM((DK, 2 * DK), BF16),
            pltpu.VMEM((NX, DK, 2 * DK), BF16),
            pltpu.VMEM((3, DK, 2 * DK), BF16),
            pltpu.VMEM((2, DK, 2 * DK), BF16),
            pltpu.VMEM((2, DK, DK), BF16),
            pltpu.VMEM((DK, DK), BF16),
            pltpu.VMEM((2, NY, DK, DK), BF16),
            sem(()), sem(()),
            sem((3,)), sem((3,)),
            sem((3,)), sem((2,)),
            sem((4,)), sem(()),
            sem((7,)), sem((7,)),
            sem((8,)), sem((8,)),
            sem((2,)),
        ],
        compiler_params=pltpu.CompilerParams(
            collective_id=1, has_side_effects=True, vmem_limit_bytes=32 * 2**20
        ),
        name="chain",
    )(gram, step_rate, decay_rate)


def read_kernel(q_ref, st_ref, gain_ref, o_ref):
    for f in range(2):
        for head in range(8):
            state = st_ref[head // 4, 2 * (head % 4) + f]
            r = jnp.dot(q_ref[head, f], state, preferred_element_type=F32)
            r = r * lax.rsqrt(jnp.mean(r * r, axis=-1, keepdims=True) + EPS)
            r = r * gain_ref[:, head * DK : (head + 1) * DK]
            o_ref[f, 0, :, head * DK : (head + 1) * DK] = r.astype(BF16)


def read(queries, states, gain):
    return pl.pallas_call(
        read_kernel,
        out_shape=jax.ShapeDtypeStruct((2, 1, 160, 1024), BF16),
        in_specs=[VM] * 3,
        out_specs=VM,
        compiler_params=pltpu.CompilerParams(vmem_limit_bytes=32 * 2**20),
        name="read",
    )(queries, states, gain)


def body(video_latents, qkv_weight, beta_weight, conv_kernel, decay_rate, step_rate, output_gain):
    queries, gram = mix(video_latents.reshape(2, 160, 1024), qkv_weight, beta_weight, conv_kernel)
    states = chain(gram, step_rate, decay_rate)
    return read(queries, states, output_gain.reshape(1, 1024))


def solution(mesh):
    placed = (P("tm", "height", None, None), P("tm", None), P(), P(), P("tm", None), P(), P())
    return jax.shard_map(
        body, mesh=mesh, in_specs=placed, out_specs=P("tm", "height", None, None), check_vma=False
    )
```

time: 1010 us -> 100 us (0.10)
  the two profiles are of different devices: /device:TPU:1 before, /device:TPU:385 now
where the time goes in v1:
time: 100 us
  Pallas kernels  96.4 us (96%)
  local copies, waits for them, and re-layouts  3.6 us (4%)
    pallas_call x1, Pallas kernels, mix(): pl.pallas_call(mix_kernel, out_shape=(jax.ShapeDtypeStruct((8, 2, 160, 12...  56.5 us
    pallas_call x1, Pallas kernels, chain(): pl.pallas_call(chain_kernel, out_shape=jax.ShapeDtypeStruct((2, NY, DK, D...  38.5 us
    unnamed x13, local copies, waits for them, and re-layouts  3.6 us

profile of v1, /device:TPU:385, one launch (start us, length us, event | category | flops | bytes accessed | tf_op | source)
XLA Modules:
  0.0 100.1 jit_solution(13943322353484599389)
XLA Ops:
  0.0 0.0 copy-start.1
  0.0 0.9 copy.8.bw_ref
  0.9 0.0 copy-done.1
  0.9 0.0 copy-start
  1.0 1.1 %copy-done = bf16[2,1,160,1024]{3,2,1,0:T(8,128)(2,1)S(1)} copy-done((bf16[2,1,160,1024]{3,2,1,0:T(8,128)(2,1)S(1)}, bf16[2,1,160,1024]{3,2,1,0:T(8,128)(2,1)}, u32[]{:S(2)}) %copy-start) | copy-done | bytes 655384
  2.0 0.0 copy-start.2
  2.0 0.9 copy-done.2
  2.9 56.5 %mix.1 = (bf16[8,2,160,128]{3,2,1,0:T(8,128)(2,1)S(1)}, f32[128,256]{1,0:T(8,128)S(1)}) custom-call(bf16[2,160,1024]{2,1,0:T(8,128)(2,1)S(1)} %bitcast.2, bf16[32,3072]{1,0:T(8,128)(2,1)S(1)} %copy-done.1, bf16[1024,8]{1,0:T(8,128)(2,1)S(1)} %copy.8.bw_ref, f32[3,3,3072]{2,1,0:T(4,128)S(1)} %copy-done.2), custom_call_target="tpu_custom_call" | custom-call | tf_op jit(solution)/shard_map/mix/pallas_call | solution.py:320
  59.4 0.0 copy-start.4
  59.5 0.0 copy-start.5
  59.5 0.7 copy-done.4
  60.1 0.0 copy-done.5
  60.1 0.0 copy-start.3
  60.1 38.5 %chain.1.st_ref = bf16[2,8,128,128]{3,2,1,0:T(8,128)(2,1)S(1)} custom-call(f32[128,256]{1,0:T(8,128)S(1)} %get-tuple-element.8.g_ref, f32[8]{0:T(128)S(1)} %copy-done.5, f32[2,8]{1,0:T(2,128)S(1)} %copy-done.4), custom_call_target="tpu_custom_call" | custom-call | tf_op jit(solution)/shard_map/chain/pallas_call | solution.py:522
  98.6 0.0 copy-done.3
  98.7 1.4 %read.1 = bf16[2,1,160,1024]{3,2,1,0:T(8,128)(2,1)} custom-call(bf16[8,2,160,128]{3,2,1,0:T(8,128)(2,1)S(1)} %get-tuple-element.7.q_ref, bf16[2,8,128,128]{3,2,1,0:T(8,128)(2,1)S(1)} %chain.1.st_ref, f32[1,1024]{1,0:T(1,128)S(1)} %bitcast.3), custom_call_target="tpu_custom_call" | custom-call | tf_op jit(solution)/shard_map/read/pallas_call | solution.py:562
Async XLA Ops:
  0.0 0.9 copy-start.1
  0.9 1.1 %copy-start = (bf16[2,1,160,1024]{3,2,1,0:T(8,128)(2,1)S(1)}, bf16[2,1,160,1024]{3,2,1,0:T(8,128)(2,1)}, u32[]{:S(2)}) copy-start(bf16[2,1,160,1024]{3,2,1,0:T(8,128)(2,1)} %param.7) | copy-start | bytes 1966084
  2.0 0.9 copy-start.2
  59.4 0.7 copy-start.4
  59.5 0.7 copy-start.5
  60.1 38.5 %copy-start.3 = (f32[1024]{0:T(1024)S(1)}, f32[1024]{0:T(1024)}, u32[]{:S(2)}) copy-start(f32[1024]{0:T(1024)} %param.13) | copy-start | bytes 12292

commit v2 on v0

v2 whole, which is shorter than its diff:
```python
import functools

import jax
import jax.numpy as jnp
from jax import lax
from jax.experimental import pallas as pl
from jax.experimental.pallas import tpu as pltpu
from jax.sharding import PartitionSpec as P

MESH = pl.DeviceIdType.MESH
EPS = 1e-06
F32 = jnp.float32
BF16 = jnp.bfloat16
NX, NZ, NY = 4, 8, 8
TOKENS = 64 * 16 * 160
DK = 128
VM = pl.BlockSpec(memory_space=pltpu.VMEM)
SM = pl.BlockSpec(memory_space=pltpu.SMEM)
ANY = pl.BlockSpec(memory_space=pl.ANY)


def place():
    t, h = lax.axis_index("tm"), lax.axis_index("height")
    return lax.rem(t, NX), lax.div(h, 2), lax.div(t, NX), lax.rem(h, 2)


def dev(x, y, z, c):
    return (z * NX + x, y * 2 + c)


def up(i, d, n):
    return lax.rem(i + d, n)


def down(i, d, n):
    return lax.rem(i + n - d, n)


def rcopy(src, dst, ssem, rsem, to):
    return pltpu.make_async_remote_copy(
        src_ref=src, dst_ref=dst, send_sem=ssem, recv_sem=rsem, device_id=to, device_id_type=MESH
    )


def signal(barrier, to):
    pl.semaphore_signal(barrier, inc=1, device_id=to, device_id_type=MESH)


def exact(a, b):
    return jnp.dot(a, b, preferred_element_type=F32, precision=lax.Precision.HIGHEST)


def inverse(system):
    ident = (
        lax.broadcasted_iota(jnp.int32, (DK, DK), 0) == lax.broadcasted_iota(jnp.int32, (DK, DK), 1)
    ).astype(F32)
    power = ident - 0.4 * system
    total = ident + power
    for _ in range(4):
        power = exact(power, power)
        total = total + exact(total, power)
    return 0.4 * total


def mix_kernel(
    x_ref, w_ref, bw_ref, ck_hbm, rate_ref, decay_ref, q_ref, st_ref,
    xe, wg, ck_ref, proj, kv, wt, beta, qbuf, part, got, own, fin, px, zin, state, cb, st,
    s_row, r_row, s_fwd, r_fwd, s_ax, r_ax, s_az, r_az, s_bz, r_bz, s_bx, r_bx, s_g, r_g, s_q, r_q, l_q, l_in,
    s_f, r_f, s_x, r_x, s_z, r_z, s_zs, r_zs, s_st, r_st, s_sib, r_sib, l_st,
):
    x, y, z, c = place()
    par, half_y = lax.rem(y, 2), lax.div(y, 2)
    sibling = dev(x, y, z, 1 - c)
    ynext, yprev = up(y, 1, NY), down(y, 1, NY)

    loads = [pltpu.make_async_copy(x_ref.at[f], xe.at[f, 2 + c], l_in.at[f]) for f in range(2)]
    for s in range(2):
        for g in range(3):
            col = pl.multiple_of(g * 1024 + (4 * par + 2 * c + s) * 128, 128)
            loads.append(
                pltpu.make_async_copy(
                    w_ref.at[:, pl.ds(col, 128)], wg.at[s, z, x, :, pl.ds(g * 128, 128)], l_in.at[2 + 3 * s + g]
                )
            )
    taps_in = pltpu.make_async_copy(ck_hbm, ck_ref, l_in.at[8])
    for cp in loads:
        cp.start()
    taps_in.start()

    barrier = pltpu.get_barrier_semaphore()
    for d in range(1, NZ):
        signal(barrier, dev(x, y, up(z, d, NZ), c))
    for d in range(1, NX):
        signal(barrier, dev(up(x, d, NX), y, z, c))
    for d in range(1, NY):
        for e in range(2):
            signal(barrier, dev(x, up(y, d, NY), z, e))
    signal(barrier, sibling)
    for cp in loads:
        cp.wait()
    pl.semaphore_wait(barrier, 25)

    zs = (dev(x, y, up(z, 1, NZ), c), dev(x, y, down(z, 1, NZ), c))

    def zsrc(dr, k):
        return down(z, k, NZ) if dr == 0 else up(z, k, NZ)

    def b_view(zz, k, dr):
        return wg.at[1, zz, x, pl.ds(16 * dr, 16)] if k == 4 else wg.at[1, zz, x]

    def b_copy(dr, k, sending):
        ref = b_view(zsrc(dr, k - 1 if sending else k), k, dr)
        return rcopy(ref, ref, s_bz.at[dr, k - 1], r_bz.at[dr, k - 1], zs[dr])

    def a_copy(dr, hf, k, sending):
        ref = wg.at[0, zsrc(dr, k - 1 if sending else k), pl.ds(2 * hf, 2)]
        return rcopy(ref, ref, s_az.at[dr, hf, k - 1], r_az.at[dr, hf, k - 1], zs[dr])

    def ax_copy(d, xx):
        ref = wg.at[0, z, xx]
        return rcopy(ref, ref, s_ax.at[d - 1], r_ax.at[d - 1], dev(up(x, d, NX), y, z, c))

    def bx_copy(d, zz, xx):
        ref = wg.at[1, zz, xx]
        return rcopy(ref, ref, s_bx.at[d - 1, zz], r_bx.at[d - 1, zz], dev(up(x, d, NX), y, z, c))

    def bx_start(zz):
        for d in (2, 1, 3):
            bx_copy(d, zz, x).start()

    for dr in range(2):
        b_copy(dr, 1, True).start()
    for d in (2, 1, 3):
        ax_copy(d, x).start()

    def row_copy(f, dr):
        to = dev(x, ynext, z, c) if dr == 0 else dev(x, yprev, z, c)
        return rcopy(xe.at[f, 2 + c], xe.at[f, 4 * dr + c], s_row.at[f, dr], r_row.at[f, dr], to)

    def fwd_copy(f, k, sending):
        core = c if sending else 1 - c
        ref = xe.at[f, 2 * k + core]
        return rcopy(ref, ref, s_fwd.at[f, k], r_fwd.at[f, k], sibling)

    for f in range(2):
        for dr in range(2):
            row_copy(f, dr).start()
    for f in range(2):
        fwd_copy(f, 1, True).start()
    bx_start(z)

    def rows_forward(f):
        for dr in range(2):
            row_copy(f, dr).wait_recv()
            fwd_copy(f, 2 * dr, True).start()

    def rows_wait(f):
        for k in range(3):
            fwd_copy(f, k, False).wait_recv()

    for d in range(1, NX):
        ax_copy(d, down(x, d, NX)).wait_recv()
    for hf in range(2):
        for dr in range(2):
            a_copy(dr, hf, 1, True).start()

    def hop(k):
        for dr in range(2):
            b_copy(dr, k, False).wait_recv()
            b_copy(dr, k + 1, True).start()
        for dr in range(2):
            bx_start(zsrc(dr, k))
        for hf in range(2):
            for dr in range(2):
                a_copy(dr, hf, k, False).wait_recv()
                if k < 3 or hf == dr:
                    a_copy(dr, hf, k + 1, True).start()

    hop(1)
    hop(2)
    rows_forward(0)
    hop(3)
    for dr in range(2):
        b_copy(dr, 4, False).wait_recv()
    bx_start(zsrc(0, 4))

    taps_in.wait()

    def gates_of(f):
        logits = lax.dot_general(
            xe[f, 1:5].reshape(640, 1024), bw_ref[...], (((1,), (1,)), ((), ())), preferred_element_type=F32
        )
        gates = jax.nn.sigmoid(logits)
        lanes = lax.broadcasted_iota(jnp.int32, (640, 8), 1)
        for s in range(2):
            picked = jnp.where(lanes == 4 * par + 2 * c + s, gates, 0.0)
            beta[f, s] = jnp.broadcast_to(jnp.sum(picked, axis=1, keepdims=True), (640, 128))

    rows_wait(0)
    gates_of(0)
    for d in range(1, NX):
        for k in range(NZ):
            bx_copy(d, k, down(x, d, NX)).wait_recv()

    low = jnp.where(y == 0, 0.0, 1.0).astype(F32)
    high = jnp.where(y == NY - 1, 0.0, 1.0).astype(F32)

    def unit_owner(slot, f):
        j = 2 * c + slot
        return 2 * j + par, f

    def step(i, carry):
        f, slot = lax.div(i, 2), 1 - lax.rem(i, 2)

        @pl.when(i == 1)
        def _():
            for dr in range(2):
                a_copy(dr, dr, 4, False).wait_recv()
            rows_forward(1)

        @pl.when(i == 2)
        def _():
            rows_wait(1)
            gates_of(1)

        proj[...] = (
            jnp.dot(
                xe[f].reshape(960, 1024), wg[slot].reshape(1024, 384), preferred_element_type=F32
            )
            .astype(BF16)
            .reshape(6, 160, 384)
        )
        ids = lax.broadcasted_iota(jnp.int32, (160, 128), 0)
        for g in range(3):
            col = pl.multiple_of(g * 1024 + (4 * par + 2 * c + slot) * 128, 128)
            taps = [[ck_ref[a, pl.ds(b, 1), pl.ds(col, 128)] for b in range(3)] for a in range(3)]
            for o in range(4):
                scale = {(0, 2): low, (1, 0): low, (2, 2): high, (3, 0): high}
                rows = [proj[o + a, :, g * 128 : (g + 1) * 128].astype(F32) for a in range(3)]
                sums = [
                    sum(
                        rows[a] * (taps[a][b] * scale[(o, a)] if (o, a) in scale else taps[a][b])
                        for a in range(3)
                    )
                    for b in range(3)
                ]
                total = (
                    jnp.where(ids > 0, pltpu.roll(sums[0], 1, 0), 0.0)
                    + sums[1]
                    + jnp.where(ids < 159, pltpu.roll(sums[2], 159, 0), 0.0)
                )
                s = total * jax.nn.sigmoid(total)
                if g < 2:
                    s = s * lax.rsqrt(jnp.sum(s * s, axis=-1, keepdims=True) + EPS)
                s = s.astype(BF16)
                if g == 0:
                    qbuf[slot, o, f] = s
                else:
                    kv[o * 160 : (o + 1) * 160, (g - 1) * 128 : g * 128] = s
                if g == 1:
                    wt[o * 160 : (o + 1) * 160, :] = (
                        beta[f, slot, o * 160 : (o + 1) * 160, :] * s.astype(F32)
                    ).astype(BF16)
        unit = lax.dot_general(
            wt[...], kv[...], (((0,), (0,)), ((), ())), preferred_element_type=F32
        ).astype(BF16)
        part[slot, f] = unit
        owner, core = unit_owner(slot, f)
        here = (owner == y) & (core == c)

        @pl.when(here)
        def _():
            got[half_y] = unit

        @pl.when(jnp.logical_not(here))
        def _():
            rcopy(
                part.at[slot, f], got.at[half_y], s_g.at[slot, f], r_g.at[half_y], dev(x, owner, z, core)
            ).start()

        return carry

    lax.fori_loop(0, 4, step, 0)

    def q_out(slot, o, send):
        head = 4 * par + 2 * c + slot
        to = {0: dev(x, yprev, z, 1), 1: dev(x, y, z, 0), 2: dev(x, y, z, 1), 3: dev(x, ynext, z, 0)}[o]

        def act(cp, local):
            if send:
                cp.start()
            elif local:
                cp.wait()
            else:
                cp.wait_send()

        far = rcopy(qbuf.at[slot, o], q_ref.at[head], s_q.at[slot, o], r_q.at[head], to)
        if o in (0, 3):
            act(far, False)
            return

        @pl.when(c == o - 1)
        def _():
            act(pltpu.make_async_copy(qbuf.at[slot, o], q_ref.at[head], l_q.at[slot]), True)

        @pl.when(c != o - 1)
        def _():
            act(far, False)

    for slot in range(2):
        for o in (0, 3, 1, 2):
            q_out(slot, o, True)

    step_size = rate_ref[4 * par + half_y] * (DK / TOKENS)
    retain = jnp.exp(-jnp.full((DK, DK), decay_ref[c, 4 * par + half_y], F32))
    summed = None
    for k in range(4):
        source_is_here = (k == half_y) & (lax.div(half_y, 2) == c)

        @pl.when(jnp.logical_not(source_is_here))
        def _():
            rcopy(got.at[k], got.at[k], s_g.at[0, 0], r_g.at[k], sibling).wait_recv()

        summed = got[k].astype(F32) if summed is None else summed + got[k].astype(F32)
    gram, written = summed[:, :DK], summed[:, DK:]
    diagonal = lax.broadcasted_iota(jnp.int32, (DK, DK), 0) == lax.broadcasted_iota(
        jnp.int32, (DK, DK), 1
    )
    system = jnp.where(diagonal, 1.0, 0.0) + (0.5 * step_size) * (gram + gram.T)
    solved = inverse(system)
    own[:, :DK] = (retain * solved).astype(BF16)
    own[:, DK:] = (retain * exact(solved, step_size * written)).astype(BF16)

    def compose(latter, earlier):
        both = jnp.dot(latter[:, :DK], earlier, preferred_element_type=F32)
        return jnp.concatenate([both[:, :DK], both[:, DK:] + latter[:, DK:].astype(F32)], axis=1).astype(BF16)

    pair = rcopy(own, fin, s_f, r_f, sibling)
    pair.start()
    pair.wait_recv()
    mine, other = own[...], fin[...]
    both = compose(jnp.where(c == 0, other, mine), jnp.where(c == 0, mine, other))
    px[x] = both

    def px_copy(d, xx):
        return rcopy(px.at[xx], px.at[xx], s_x.at[d - 1], r_x.at[d - 1], dev(up(x, d, NX), y, z, c))

    for d in (2, 1, 3):
        px_copy(d, x).start()
    for d in (1, 3, 2):
        px_copy(d, down(x, d, NX)).wait_recv()
    first = compose(px[1], px[0])
    line = compose(compose(px[3], px[2]), first)
    zin[0, z] = line[:, :DK]
    zin[1, z] = line[:, DK:]

    def z_copy(e):
        return rcopy(zin.at[c, z], zin.at[c, z], s_z.at[e - 1], r_z.at[z], dev(x, y, z + e, c))

    def zs_copy(k, sending):
        core = c if sending else 1 - c
        return rcopy(zin.at[core, k], zin.at[core, k], s_zs.at[k], r_zs.at[k], sibling)

    for e in range(NZ - 1, 0, -1):

        @pl.when(z + e < NZ)
        def _():
            z_copy(e).start()

    third = compose(px[2], first)
    current = jnp.where(c == 0, mine, both)
    before = jnp.where(x == 1, px[0], jnp.where(x == 2, first, third))
    fin[...] = jnp.where(x == 0, current, compose(current, before))

    for e in range(1, NZ):

        @pl.when(z >= e)
        def _():
            k = z - e
            rcopy(zin.at[c, k], zin.at[c, k], s_z.at[0], r_z.at[k], sibling).wait_recv()
            zs_copy(k, True).start()

    for k in range(NZ - 1):

        @pl.when(k < z)
        def _():
            zs_copy(k, False).wait_recv()
            if k == 0:
                state[...] = zin[1, 0].astype(F32)
            else:
                state[...] = jnp.dot(
                    zin[0, k], state[...].astype(BF16), preferred_element_type=F32
                ) + zin[1, k].astype(F32)

    @pl.when(z == 0)
    def _():
        cb[...] = fin[:, DK:]

    @pl.when(z > 0)
    def _():
        cb[...] = (
            jnp.dot(fin[:, :DK], state[...].astype(BF16), preferred_element_type=F32)
            + fin[:, DK:].astype(F32)
        ).astype(BF16)

    def sib_copy(k, sending):
        core = c if sending else 1 - c
        return rcopy(st.at[core, k], st.at[core, k], s_sib.at[k], r_sib.at[k], sibling)

    def st_copy(d, yy):
        return rcopy(cb, st.at[c, yy], s_st.at[d - 1], r_st.at[d - 1], dev(x, up(y, d, NY), z, c))

    for d in (4, 3, 5, 2, 6, 1, 7):
        st_copy(d, y).start()
    st[c, y] = cb[...]
    sib_copy(y, True).start()
    for d in (1, 7, 2, 6, 3, 5, 4):
        yy = down(y, d, NY)
        st_copy(d, yy).wait_recv()
        sib_copy(yy, True).start()
    mine_out = pltpu.make_async_copy(st.at[c], st_ref.at[c], l_st.at[0])
    mine_out.start()
    for k in range(NY):
        sib_copy(k, False).wait_recv()
    other_out = pltpu.make_async_copy(st.at[1 - c], st_ref.at[1 - c], l_st.at[1])
    other_out.start()

    for slot in range(2):
        for o in range(4):
            q_out(slot, o, False)
        head = 4 * par + 2 * (1 - c) + slot
        rcopy(qbuf.at[slot, 0], q_ref.at[head], s_q.at[slot, 0], r_q.at[head], sibling).wait_recv()
    for k in range(4):
        head = 4 * (1 - par) + k
        rcopy(qbuf.at[0, 0], q_ref.at[head], s_q.at[0, 0], r_q.at[head], sibling).wait_recv()
    for slot in range(2):
        for f in range(2):
            owner, core = unit_owner(slot, f)

            @pl.when(jnp.logical_not((owner == y) & (core == c)))
            def _():
                rcopy(part.at[slot, f], got.at[0], s_g.at[slot, f], r_g.at[0], sibling).wait_send()

    for dr in range(2):
        for k in range(1, 5):
            b_copy(dr, k, True).wait_send()
            for hf in range(2):
                if k < 4 or hf == dr:
                    a_copy(dr, hf, k, True).wait_send()
    for d in range(1, NX):
        ax_copy(d, x).wait_send()
        px_copy(d, x).wait_send()
        for k in range(NZ):
            bx_copy(d, k, x).wait_send()
    for f in range(2):
        for dr in range(2):
            row_copy(f, dr).wait_send()
        for k in range(3):
            fwd_copy(f, k, True).wait_send()
    pair.wait_send()
    for e in range(1, NZ):

        @pl.when(z + e < NZ)
        def _():
            z_copy(e).wait_send()

    for k in range(NZ - 1):

        @pl.when(k < z)
        def _():
            zs_copy(k, True).wait_send()

    for d in range(1, NY):
        st_copy(d, y).wait_send()
    for k in range(NY):
        sib_copy(k, True).wait_send()
    mine_out.wait()
    other_out.wait()


def mix(latents, weight, beta_rows, conv_kernel, step_rate, decay_rate):
    sem = pltpu.SemaphoreType.DMA
    return pl.pallas_call(
        mix_kernel,
        out_shape=(
            jax.ShapeDtypeStruct((8, 2, 160, DK), BF16),
            jax.ShapeDtypeStruct((2, NY, DK, DK), BF16),
        ),
        in_specs=[ANY, ANY, VM, ANY, SM, SM],
        out_specs=(ANY, ANY),
        scratch_shapes=[
            pltpu.VMEM((2, 6, 160, 1024), BF16),
            pltpu.VMEM((2, NZ, NX, 32, 384), BF16),
            pltpu.VMEM((3, 3, 3072), F32),
            pltpu.VMEM((6, 160, 384), BF16),
            pltpu.VMEM((640, 256), BF16),
            pltpu.VMEM((640, DK), BF16),
            pltpu.VMEM((2, 2, 640, DK), F32),
            pltpu.VMEM((2, 4, 2, 160, DK), BF16),
            pltpu.VMEM((2, 2, DK, 2 * DK), BF16),
            pltpu.VMEM((4, DK, 2 * DK), BF16),
            pltpu.VMEM((DK, 2 * DK), BF16),
            pltpu.VMEM((DK, 2 * DK), BF16),
            pltpu.VMEM((NX, DK, 2 * DK), BF16),
            pltpu.VMEM((2, NZ, DK, DK), BF16),
            pltpu.VMEM((DK, DK), F32),
            pltpu.VMEM((DK, DK), BF16),
            pltpu.VMEM((2, NY, DK, DK), BF16),
            sem((2, 2)), sem((2, 2)), sem((2, 3)), sem((2, 3)),
            sem((3,)), sem((3,)), sem((2, 2, 4)), sem((2, 2, 4)),
            sem((2, 4)), sem((2, 4)), sem((3, 8)), sem((3, 8)),
            sem((2, 2)), sem((4,)), sem((2, 4)), sem((8,)), sem((2,)), sem((9,)),
            sem(()), sem(()), sem((3,)), sem((3,)),
            sem((7,)), sem((8,)), sem((8,)), sem((8,)),
            sem((7,)), sem((7,)), sem((8,)), sem((8,)), sem((2,)),
        ],
        compiler_params=pltpu.CompilerParams(
            collective_id=0, has_side_effects=True, vmem_limit_bytes=56 * 2**20
        ),
        name="mix",
    )(latents, weight, beta_rows, conv_kernel, step_rate, decay_rate)


def read_kernel(q_ref, st_ref, gain_ref, o_ref):
    for f in range(2):
        for head in range(8):
            state = st_ref[f, 2 * (head % 4) + head // 4]
            r = jnp.dot(q_ref[head, f], state, preferred_element_type=F32)
            r = r * lax.rsqrt(jnp.mean(r * r, axis=-1, keepdims=True) + EPS)
            r = r * gain_ref[:, head * DK : (head + 1) * DK]
            o_ref[f, 0, :, head * DK : (head + 1) * DK] = r.astype(BF16)


def read(queries, states, gain):
    return pl.pallas_call(
        read_kernel,
        out_shape=jax.ShapeDtypeStruct((2, 1, 160, 1024), BF16),
        in_specs=[VM] * 3,
        out_specs=VM,
        compiler_params=pltpu.CompilerParams(vmem_limit_bytes=32 * 2**20),
        name="read",
    )(queries, states, gain)


def body(video_latents, qkv_weight, beta_weight, conv_kernel, decay_rate, step_rate, output_gain):
    queries, states = mix(
        video_latents.reshape(2, 160, 1024), qkv_weight, beta_weight.T, conv_kernel, step_rate, decay_rate
    )
    return read(queries, states, output_gain.reshape(1, 1024))


def solution(mesh):
    placed = (P("tm", "height", None, None), P("tm", None), P(), P(), P("tm", None), P(), P())
    return jax.shard_map(
        body, mesh=mesh, in_specs=placed, out_specs=P("tm", "height", None, None), check_vma=False
    )
```

time: 1010 us -> 75.5 us (0.07)
  the two profiles are of different devices: /device:TPU:1 before, /device:TPU:65 now
where the time goes in v2:
time: 75.5 us; the launch traced here: 75.3 us
  Pallas kernels  73.1 us (97%)
  local copies, waits for them, and re-layouts  2.13 us (3%)
    pallas_call x1, Pallas kernels, mix(): pl.pallas_call(mix_kernel, out_shape=(jax.ShapeDtypeStruct((8, 2, 160, DK...  71.7 us
    unnamed x6, local copies, waits for them, and re-layouts  2.13 us

profile of v2, /device:TPU:65, one launch (start us, length us, event | category | flops | bytes accessed | tf_op | source)
XLA Modules:
  0.0 75.3 jit_solution(3010179015673842186)
XLA Ops:
  0.0 0.0 copy-start.2
  0.0 71.7 %mix.1 = (bf16[8,2,160,128]{3,2,1,0:T(8,128)(2,1)}, bf16[2,8,128,128]{3,2,1,0:T(8,128)(2,1)}) custom-call(bf16[2,160,1024]{2,1,0:T(8,128)(2,1)} %bitcast.4, bf16[32,3072]{1,0:T(8,128)(2,1)} %w_ref.1, bf16[8,1024]{1,0:T(8,128)(2,1)} %bitcast.5, f32[3,3,3072]{2,1,0:T(4,128)} %ck_hbm.1, f32[8]{0:T(128)} %rate_ref.1, f32[2,8]{1,0:T(2,128)} %decay_ref.1), custom_call_target="tpu_custom_call" | custom-call | tf_op jit(solution)/shard_map/mix/pallas_call | solution.py:483
  71.7 0.0 copy-done.2
  71.7 0.0 copy-start
  71.7 1.1 %copy-done = bf16[8,2,160,128]{3,2,1,0:T(8,128)(2,1)S(1)} copy-done((bf16[8,2,160,128]{3,2,1,0:T(8,128)(2,1)S(1)}, bf16[8,2,160,128]{3,2,1,0:T(8,128)(2,1)}, u32[]{:S(2)}) %copy-start) | copy-done | bytes 655384
  72.8 0.0 copy-start.1
  72.8 1.0 %copy-done.1 = bf16[2,8,128,128]{3,2,1,0:T(8,128)(2,1)S(1)} copy-done((bf16[2,8,128,128]{3,2,1,0:T(8,128)(2,1)S(1)}, bf16[2,8,128,128]{3,2,1,0:T(8,128)(2,1)}, u32[]{:S(2)}) %copy-start.1) | copy-done | bytes 524312
  73.8 1.4 %read.1 = bf16[2,1,160,1024]{3,2,1,0:T(8,128)(2,1)} custom-call(bf16[8,2,160,128]{3,2,1,0:T(8,128)(2,1)S(1)} %copy-done, bf16[2,8,128,128]{3,2,1,0:T(8,128)(2,1)S(1)} %copy-done.1, f32[1,1024]{1,0:T(1,128)S(1)} %bitcast.3), custom_call_target="tpu_custom_call" | custom-call | tf_op jit(solution)/shard_map/read/pallas_call | solution.py:535
Async XLA Ops:
  0.0 71.7 %copy-start.2 = (f32[1024]{0:T(1024)S(1)}, f32[1024]{0:T(1024)}, u32[]{:S(2)}) copy-start(f32[1024]{0:T(1024)} %param.13) | copy-start | bytes 12292
  71.7 1.1 %copy-start = (bf16[8,2,160,128]{3,2,1,0:T(8,128)(2,1)S(1)}, bf16[8,2,160,128]{3,2,1,0:T(8,128)(2,1)}, u32[]{:S(2)}) copy-start(bf16[8,2,160,128]{3,2,1,0:T(8,128)(2,1)} %get-tuple-element.7.q_ref) | copy-start | bytes 1966084
  72.8 1.0 %copy-start.1 = (bf16[2,8,128,128]{3,2,1,0:T(8,128)(2,1)S(1)}, bf16[2,8,128,128]{3,2,1,0:T(8,128)(2,1)}, u32[]{:S(2)}) copy-start(bf16[2,8,128,128]{3,2,1,0:T(8,128)(2,1)} %get-tuple-element.8.st_ref) | copy-start | bytes 1572868

commit v3 on v2

v3 whole, which is shorter than its diff:
```python
import functools

import jax
import jax.numpy as jnp
from jax import lax
from jax.experimental import pallas as pl
from jax.experimental.pallas import tpu as pltpu
from jax.sharding import PartitionSpec as P

MESH = pl.DeviceIdType.MESH
EPS = 1e-06
F32 = jnp.float32
BF16 = jnp.bfloat16
NX, NZ, NY = 4, 8, 8
TOKENS = 64 * 16 * 160
DK = 128
VM = pl.BlockSpec(memory_space=pltpu.VMEM)
SM = pl.BlockSpec(memory_space=pltpu.SMEM)
ANY = pl.BlockSpec(memory_space=pl.ANY)


def place():
    t, h = lax.axis_index("tm"), lax.axis_index("height")
    return lax.rem(t, NX), lax.div(h, 2), lax.div(t, NX), lax.rem(h, 2)


def dev(x, y, z, c):
    return (z * NX + x, y * 2 + c)


def up(i, d, n):
    return lax.rem(i + d, n)


def down(i, d, n):
    return lax.rem(i + n - d, n)


def rcopy(src, dst, ssem, rsem, to):
    return pltpu.make_async_remote_copy(
        src_ref=src, dst_ref=dst, send_sem=ssem, recv_sem=rsem, device_id=to, device_id_type=MESH
    )


def signal(barrier, to):
    pl.semaphore_signal(barrier, inc=1, device_id=to, device_id_type=MESH)


def halves(a):
    high = a.astype(BF16)
    return high, (a - high.astype(F32)).astype(BF16)


def close(a, b):
    a_high, a_low = halves(a)
    b_high, b_low = halves(b)
    both = jnp.concatenate([a_high, a_low], axis=1)
    return jnp.dot(
        both, jnp.concatenate([b_high, b_high], axis=0), preferred_element_type=F32
    ) + jnp.dot(a_high, b_low, preferred_element_type=F32)


def inverse(system, ident):
    power = ident - 0.4 * system
    total = ident + power
    power = close(power, power)
    for _ in range(3):
        stacked = close(jnp.concatenate([power, total], axis=0), power)
        power, total = stacked[:DK], total + stacked[DK:]
    return 0.4 * (total + close(total, power))


def mix_kernel(
    x_ref, w_ref, bw_ref, ck_hbm, gain_ref, rate_ref, decay_ref, o_ref,
    xe, wg, ck_ref, proj, kv, wt, beta, qbuf, q_ref, part, got, own, fin, px, zin, state, cb, st,
    s_row, r_row, s_fwd, r_fwd, s_wz, r_wz, s_wx, r_wx, s_g, r_g, s_q, r_q, l_q, l_in,
    s_f, r_f, s_x, r_x, s_z, r_z, s_zs, r_zs, s_st, r_st, s_sib, r_sib,
):
    x, y, z, c = place()
    par, half_y = lax.rem(y, 2), lax.div(y, 2)
    sibling = dev(x, y, z, 1 - c)
    ynext, yprev = up(y, 1, NY), down(y, 1, NY)

    loads = [pltpu.make_async_copy(x_ref.at[f], xe.at[f, 2 + c], l_in.at[f]) for f in range(2)]
    for s in range(2):
        for g in range(3):
            col = pl.multiple_of(g * 1024 + (4 * par + 2 * c + s) * 128, 128)
            block, lane = (2, s * 128) if g == 0 else (s, (g - 1) * 128)
            loads.append(
                pltpu.make_async_copy(
                    w_ref.at[:, pl.ds(col, 128)], wg.at[block, z, x, :, pl.ds(lane, 128)], l_in.at[2 + 3 * s + g]
                )
            )
    taps_in = pltpu.make_async_copy(ck_hbm, ck_ref, l_in.at[8])
    for cp in loads:
        cp.start()
    taps_in.start()

    barrier = pltpu.get_barrier_semaphore()
    for d in range(1, NZ):
        signal(barrier, dev(x, y, up(z, d, NZ), c))
    for d in range(1, NX):
        signal(barrier, dev(up(x, d, NX), y, z, c))
    for d in range(1, NY):
        for e in range(2):
            signal(barrier, dev(x, up(y, d, NY), z, e))
    signal(barrier, sibling)
    for cp in loads:
        cp.wait()
    pl.semaphore_wait(barrier, 25)

    def wz_copy(n, d, zz):
        ref = wg.at[n, zz, x]
        return rcopy(ref, ref, s_wz.at[n, d - 1], r_wz.at[n, d - 1], dev(x, y, up(z, d, NZ), c))

    def wx_copy(n, d, zz, xx):
        ref = wg.at[n, zz, xx]
        return rcopy(ref, ref, s_wx.at[n, d - 1, zz], r_wx.at[n, d - 1, zz], dev(up(x, d, NX), y, z, c))

    def wx_start(n, zz):
        for d in (2, 1, 3):
            wx_copy(n, d, zz, x).start()

    def wz_start(n):
        for d in (4, 3, 5, 2, 6, 1, 7):
            wz_copy(n, d, z).start()

    def weights_forward(n):
        for d in (1, 7, 2, 6, 3, 5, 4):
            zz = down(z, d, NZ)
            wz_copy(n, d, zz).wait_recv()
            wx_start(n, zz)

    def weights_wait(n):
        for d in range(1, NX):
            for k in range(NZ):
                wx_copy(n, d, k, down(x, d, NX)).wait_recv()

    def row_copy(f, dr):
        to = dev(x, ynext, z, c) if dr == 0 else dev(x, yprev, z, c)
        return rcopy(xe.at[f, 2 + c], xe.at[f, 4 * dr + c], s_row.at[f, dr], r_row.at[f, dr], to)

    def fwd_copy(f, k, sending):
        core = c if sending else 1 - c
        ref = xe.at[f, 2 * k + core]
        return rcopy(ref, ref, s_fwd.at[f, k], r_fwd.at[f, k], sibling)

    wz_start(0)
    wx_start(0, z)
    for f in range(2):
        for dr in range(2):
            row_copy(f, dr).start()
        fwd_copy(f, 1, True).start()
        wz_start(1 + f)
    for n in (1, 2):
        wx_start(n, z)

    def rows_forward(f):
        for dr in range(2):
            row_copy(f, dr).wait_recv()
            fwd_copy(f, 2 * dr, True).start()

    def rows_wait(f):
        for k in range(3):
            fwd_copy(f, k, False).wait_recv()

    weights_forward(0)
    weights_forward(1)
    rows_forward(0)
    weights_forward(2)
    taps_in.wait()

    def gates_of(f):
        logits = lax.dot_general(
            xe[f, 1:5].reshape(640, 1024), bw_ref[...], (((1,), (1,)), ((), ())), preferred_element_type=F32
        )
        gates = jax.nn.sigmoid(logits)
        lanes = lax.broadcasted_iota(jnp.int32, (640, 8), 1)
        for s in range(2):
            picked = jnp.where(lanes == 4 * par + 2 * c + s, gates, 0.0)
            beta[f, s] = jnp.broadcast_to(jnp.sum(picked, axis=1, keepdims=True), (640, 128))

    rows_wait(0)
    gates_of(0)
    weights_wait(0)

    low = jnp.where(y == 0, 0.0, 1.0).astype(F32)
    high = jnp.where(y == NY - 1, 0.0, 1.0).astype(F32)

    def unit_owner(slot, f):
        j = 2 * c + slot
        return 2 * j + par, f

    ids = lax.broadcasted_iota(jnp.int32, (160, 128), 0)

    def project(f, n):
        proj[...] = (
            jnp.dot(
                xe[f].reshape(960, 1024), wg[n].reshape(1024, 256), preferred_element_type=F32
            )
            .astype(BF16)
            .reshape(6, 160, 256)
        )

    def stream(part_of, head, half, o):
        col = pl.multiple_of(part_of * 1024 + head * 128, 128)
        scale = {(0, 2): low, (1, 0): low, (2, 2): high, (3, 0): high}
        sums = [None] * 3
        for a in range(3):
            row = proj[o + a, :, half * 128 : (half + 1) * 128].astype(F32)
            for b in range(3):
                tap = ck_ref[a, pl.ds(b, 1), pl.ds(col, 128)]
                tap = tap * scale[(o, a)] if (o, a) in scale else tap
                sums[b] = row * tap if a == 0 else sums[b] + row * tap
        total = (
            jnp.where(ids > 0, pltpu.roll(sums[0], 1, 0), 0.0)
            + sums[1]
            + jnp.where(ids < 159, pltpu.roll(sums[2], 159, 0), 0.0)
        )
        return total * jax.nn.sigmoid(total)

    def normed(s):
        return (s * lax.rsqrt(jnp.sum(s * s, axis=-1, keepdims=True) + EPS)).astype(BF16)

    def step(i, carry):
        f, slot = lax.div(i, 2), lax.rem(i, 2)

        @pl.when(i == 1)
        def _():
            weights_wait(1)

        @pl.when(i == 2)
        def _():
            rows_forward(1)
            rows_wait(1)
            gates_of(1)

        project(f, slot)
        head = 4 * par + 2 * c + slot
        for o in range(4):
            here = slice(o * 160, (o + 1) * 160)
            key = normed(stream(1, head, 0, o))
            kv[here, :DK] = key
            wt[here, :] = (beta[f, slot, here, :] * key.astype(F32)).astype(BF16)
            kv[here, DK:] = stream(2, head, 1, o).astype(BF16)
        unit = lax.dot_general(
            wt[...], kv[...], (((0,), (0,)), ((), ())), preferred_element_type=F32
        ).astype(BF16)
        part[slot, f] = unit
        owner, core = unit_owner(slot, f)
        here = (owner == y) & (core == c)

        @pl.when(here)
        def _():
            got[half_y] = unit

        @pl.when(jnp.logical_not(here))
        def _():
            rcopy(
                part.at[slot, f], got.at[half_y], s_g.at[slot, f], r_g.at[half_y], dev(x, owner, z, core)
            ).start()

        return carry

    lax.fori_loop(0, 4, step, 0)

    weights_wait(2)

    def query(f, carry):
        project(f, 2)
        for slot in range(2):
            for o in range(4):
                qbuf[slot, o, f] = normed(stream(0, 4 * par + 2 * c + slot, slot, o))
        return carry

    lax.fori_loop(0, 2, query, 0)

    def q_out(slot, o, send):
        head = 4 * par + 2 * c + slot
        to = {0: dev(x, yprev, z, 1), 1: dev(x, y, z, 0), 2: dev(x, y, z, 1), 3: dev(x, ynext, z, 0)}[o]

        def far():
            cp = rcopy(qbuf.at[slot, o], q_ref.at[head], s_q.at[slot, o], r_q.at[head], to)
            cp.start() if send else cp.wait_send()

        if o in (0, 3):
            far()
            return
        pl.when(c != o - 1)(far)
        if send:

            @pl.when(c == o - 1)
            def _():
                pltpu.make_async_copy(qbuf.at[slot, o], q_ref.at[head], l_q.at[slot]).start()

    for slot in range(2):
        for o in (0, 3, 1, 2):
            q_out(slot, o, True)

    step_size = rate_ref[4 * par + half_y] * (DK / TOKENS)
    retain = jnp.exp(-jnp.full((DK, DK), decay_ref[c, 4 * par + half_y], F32))
    summed = None
    for k in range(4):
        source_is_here = (k == half_y) & (lax.div(half_y, 2) == c)

        @pl.when(jnp.logical_not(source_is_here))
        def _():
            rcopy(got.at[k], got.at[k], s_g.at[0, 0], r_g.at[k], sibling).wait_recv()

        summed = got[k].astype(F32) if summed is None else summed + got[k].astype(F32)
    gram, written = summed[:, :DK], summed[:, DK:]
    diagonal = lax.broadcasted_iota(jnp.int32, (DK, DK), 0) == lax.broadcasted_iota(
        jnp.int32, (DK, DK), 1
    )
    ident = jnp.where(diagonal, 1.0, 0.0)
    solved = inverse(ident + (0.5 * step_size) * (gram + gram.T), ident)
    own[:, :DK] = (retain * solved).astype(BF16)
    own[:, DK:] = (retain * close(solved, step_size * written)).astype(BF16)

    def compose(latter, earlier):
        both = jnp.dot(latter[:, :DK], earlier, preferred_element_type=F32)
        return jnp.concatenate([both[:, :DK], both[:, DK:] + latter[:, DK:].astype(F32)], axis=1).astype(BF16)

    pair = rcopy(own, fin, s_f, r_f, sibling)
    pair.start()
    pair.wait_recv()
    mine, other = own[...], fin[...]
    both = compose(jnp.where(c == 0, other, mine), jnp.where(c == 0, mine, other))
    px[x] = both

    def px_copy(d, xx):
        return rcopy(px.at[xx], px.at[xx], s_x.at[d - 1], r_x.at[d - 1], dev(up(x, d, NX), y, z, c))

    for d in (2, 1, 3):
        px_copy(d, x).start()
    for d in (1, 3, 2):
        px_copy(d, down(x, d, NX)).wait_recv()
    first = compose(px[1], px[0])
    line = compose(compose(px[3], px[2]), first)
    zin[0, z] = line[:, :DK]
    zin[1, z] = line[:, DK:]

    def z_copy(e):
        return rcopy(zin.at[c, z], zin.at[c, z], s_z.at[e - 1], r_z.at[z], dev(x, y, z + e, c))

    def zs_copy(k, sending):
        core = c if sending else 1 - c
        return rcopy(zin.at[core, k], zin.at[core, k], s_zs.at[k], r_zs.at[k], sibling)

    for e in range(NZ - 1, 0, -1):

        @pl.when(z + e < NZ)
        def _():
            z_copy(e).start()

    third = compose(px[2], first)
    current = jnp.where(c == 0, mine, both)
    before = jnp.where(x == 1, px[0], jnp.where(x == 2, first, third))
    fin[...] = jnp.where(x == 0, current, compose(current, before))

    for e in range(1, NZ):

        @pl.when(z >= e)
        def _():
            k = z - e
            rcopy(zin.at[c, k], zin.at[c, k], s_z.at[0], r_z.at[k], sibling).wait_recv()
            zs_copy(k, True).start()

    for k in range(NZ - 1):

        @pl.when(k < z)
        def _():
            zs_copy(k, False).wait_recv()
            if k == 0:
                state[...] = zin[1, 0].astype(F32)
            else:
                state[...] = jnp.dot(
                    zin[0, k], state[...].astype(BF16), preferred_element_type=F32
                ) + zin[1, k].astype(F32)

    @pl.when(z == 0)
    def _():
        cb[...] = fin[:, DK:]

    @pl.when(z > 0)
    def _():
        cb[...] = (
            jnp.dot(fin[:, :DK], state[...].astype(BF16), preferred_element_type=F32)
            + fin[:, DK:].astype(F32)
        ).astype(BF16)

    def sib_copy(k, sending):
        core = c if sending else 1 - c
        return rcopy(st.at[core, k], st.at[core, k], s_sib.at[k], r_sib.at[k], sibling)

    def st_copy(d, yy):
        return rcopy(cb, st.at[c, yy], s_st.at[d - 1], r_st.at[d - 1], dev(x, up(y, d, NY), z, c))

    for d in (4, 3, 5, 2, 6, 1, 7):
        st_copy(d, y).start()
    st[c, y] = cb[...]
    sib_copy(y, True).start()

    for slot in range(2):
        head = 4 * par + 2 * (1 - c) + slot
        rcopy(qbuf.at[slot, 0], q_ref.at[head], s_q.at[slot, 0], r_q.at[head], sibling).wait_recv()
        pltpu.make_async_copy(qbuf.at[slot, 0], q_ref.at[4 * par + 2 * c + slot], l_q.at[slot]).wait()
    for k in range(4):
        head = 4 * (1 - par) + k
        rcopy(qbuf.at[0, 0], q_ref.at[head], s_q.at[0, 0], r_q.at[head], sibling).wait_recv()

    def read(f, k):
        head = 4 * lax.rem(k, 2) + lax.div(k, 2)
        r = jnp.dot(q_ref[head, f], st[f, k], preferred_element_type=F32)
        r = r * lax.rsqrt(jnp.mean(r * r, axis=-1, keepdims=True) + EPS)
        lane = pl.ds(pl.multiple_of(head * DK, DK), DK)
        o_ref[f, 0, :, lane] = (r * gain_ref[:, lane]).astype(BF16)

    read(c, y)
    for d in (1, 7, 2, 6, 3, 5, 4):
        yy = down(y, d, NY)
        st_copy(d, yy).wait_recv()
        sib_copy(yy, True).start()
        read(c, yy)
    for d in (0, 1, 7, 2, 6, 3, 5, 4):
        yy = down(y, d, NY)
        sib_copy(yy, False).wait_recv()
        read(1 - c, yy)

    for slot in range(2):
        for o in range(4):
            q_out(slot, o, False)
    for slot in range(2):
        for f in range(2):
            owner, core = unit_owner(slot, f)

            @pl.when(jnp.logical_not((owner == y) & (core == c)))
            def _():
                rcopy(part.at[slot, f], got.at[0], s_g.at[slot, f], r_g.at[0], sibling).wait_send()

    for n in range(3):
        for d in range(1, NZ):
            wz_copy(n, d, z).wait_send()
        for d in range(1, NX):
            for k in range(NZ):
                wx_copy(n, d, k, x).wait_send()
    for d in range(1, NX):
        px_copy(d, x).wait_send()
    for f in range(2):
        for dr in range(2):
            row_copy(f, dr).wait_send()
        for k in range(3):
            fwd_copy(f, k, True).wait_send()
    pair.wait_send()
    for e in range(1, NZ):

        @pl.when(z + e < NZ)
        def _():
            z_copy(e).wait_send()

    for k in range(NZ - 1):

        @pl.when(k < z)
        def _():
            zs_copy(k, True).wait_send()

    for d in range(1, NY):
        st_copy(d, y).wait_send()
    for k in range(NY):
        sib_copy(k, True).wait_send()


def mix(latents, weight, beta_rows, conv_kernel, gain, step_rate, decay_rate):
    sem = pltpu.SemaphoreType.DMA
    return pl.pallas_call(
        mix_kernel,
        out_shape=jax.ShapeDtypeStruct((2, 1, 160, 1024), BF16),
        in_specs=[ANY, ANY, VM, ANY, VM, SM, SM],
        out_specs=VM,
        scratch_shapes=[
            pltpu.VMEM((2, 6, 160, 1024), BF16),
            pltpu.VMEM((3, NZ, NX, 32, 256), BF16),
            pltpu.VMEM((3, 3, 3072), F32),
            pltpu.VMEM((6, 160, 256), BF16),
            pltpu.VMEM((640, 256), BF16),
            pltpu.VMEM((640, DK), BF16),
            pltpu.VMEM((2, 2, 640, DK), F32),
            pltpu.VMEM((2, 4, 2, 160, DK), BF16),
            pltpu.VMEM((8, 2, 160, DK), BF16),
            pltpu.VMEM((2, 2, DK, 2 * DK), BF16),
            pltpu.VMEM((4, DK, 2 * DK), BF16),
            pltpu.VMEM((DK, 2 * DK), BF16),
            pltpu.VMEM((DK, 2 * DK), BF16),
            pltpu.VMEM((NX, DK, 2 * DK), BF16),
            pltpu.VMEM((2, NZ, DK, DK), BF16),
            pltpu.VMEM((DK, DK), F32),
            pltpu.VMEM((DK, DK), BF16),
            pltpu.VMEM((2, NY, DK, DK), BF16),
            sem((2, 2)), sem((2, 2)), sem((2, 3)), sem((2, 3)),
            sem((3, 7)), sem((3, 7)), sem((3, 3, 8)), sem((3, 3, 8)),
            sem((2, 2)), sem((4,)), sem((2, 4)), sem((8,)), sem((2,)), sem((9,)),
            sem(()), sem(()), sem((3,)), sem((3,)),
            sem((7,)), sem((8,)), sem((8,)), sem((8,)),
            sem((7,)), sem((7,)), sem((8,)), sem((8,)),
        ],
        compiler_params=pltpu.CompilerParams(
            collective_id=0, has_side_effects=True, vmem_limit_bytes=56 * 2**20
        ),
        name="mix",
    )(latents, weight, beta_rows, conv_kernel, gain, step_rate, decay_rate)


def body(video_latents, qkv_weight, beta_weight, conv_kernel, decay_rate, step_rate, output_gain):
    return mix(
        video_latents.reshape(2, 160, 1024), qkv_weight, beta_weight.T, conv_kernel,
        output_gain.reshape(1, 1024), step_rate, decay_rate,
    )


def solution(mesh):
    placed = (P("tm", "height", None, None), P("tm", None), P(), P(), P("tm", None), P(), P())
    return jax.shard_map(
        body, mesh=mesh, in_specs=placed, out_specs=P("tm", "height", None, None), check_vma=False
    )
```

time: 75.5 us -> 74 us (0.980)
  Pallas kernels: 73.1 us -> 71.8 us
    pallas_call x2 -> x1, Pallas kernels: 73.1 us -> 71.8 us  [mix(): pl.pallas_call(mix_kernel, out_shape=jax.ShapeDtypeStruct((2, 1, 160, 102...]
    unnamed x6 -> x1, local copies, waits for them, and re-layouts: 2.13 us -> 1.97 us
where the time goes in v3:
time: 74 us; the launch traced here: 73.7 us
  Pallas kernels  71.8 us (97%)
  local copies, waits for them, and re-layouts  1.97 us (3%)
    pallas_call x1, Pallas kernels, mix(): pl.pallas_call(mix_kernel, out_shape=jax.ShapeDtypeStruct((2, 1, 160, 102...  71.8 us
    unnamed x1, local copies, waits for them, and re-layouts  1.97 us

profile of v3, /device:TPU:65, one launch (start us, length us, event | category | flops | bytes accessed | tf_op | source)
XLA Modules:
  0.0 73.7 jit_solution(18295533939879163346)
XLA Ops:
  0.0 71.8 %mix.1 = bf16[2,1,160,1024]{3,2,1,0:T(8,128)(2,1)} custom-call(bf16[2,160,1024]{2,1,0:T(8,128)(2,1)} %bitcast.3, bf16[32,3072]{1,0:T(8,128)(2,1)} %w_ref.1, bf16[8,1024]{1,0:T(8,128)(2,1)} %bitcast.4, f32[3,3,3072]{2,1,0:T(4,128)} %ck_hbm.1, f32[1,1024]{1,0:T(1,128)} %bitcast.5, f32[8]{0:T(128)} %rate_ref.1, f32[2,8]{1,0:T(2,128)} %decay_ref.1), custom_call_target="tpu_custom_call" | custom-call | tf_op jit(solution)/shard_map/mix/pallas_call | solution.py:475
  71.8 2.0 %copy.9 = bf16[2,1,160,1024]{3,2,1,0:T(8,128)(2,1)} copy(bf16[2,1,160,1024]{3,2,1,0:T(8,128)(2,1)} %mix.1) | data formatting | bytes 1310720

commit v4 on v3

--- a/solution.py
+++ b/solution.py
@@ -122,7 +122,7 @@
             wx_copy(n, d, zz, x).start()
 
     def wz_start(n):
-        for d in (4, 3, 5, 2, 6, 1, 7):
+        for d in (1, 7, 2, 6, 3, 5, 4):
             wz_copy(n, d, z).start()
 
     def weights_forward(n):
@@ -136,38 +136,46 @@
             for k in range(NZ):
                 wx_copy(n, d, k, down(x, d, NX)).wait_recv()
 
-    def row_copy(f, dr):
+    def row_copy(f, dr, hf):
         to = dev(x, ynext, z, c) if dr == 0 else dev(x, yprev, z, c)
-        return rcopy(xe.at[f, 2 + c], xe.at[f, 4 * dr + c], s_row.at[f, dr], r_row.at[f, dr], to)
-
-    def fwd_copy(f, k, sending):
+        cols = pl.ds(80 * hf, 80)
+        return rcopy(
+            xe.at[f, 2 + c, cols], xe.at[f, 4 * dr + c, cols], s_row.at[f, dr, hf], r_row.at[f, dr, hf], to
+        )
+
+    def fwd_copy(f, k, hf, sending):
         core = c if sending else 1 - c
-        ref = xe.at[f, 2 * k + core]
-        return rcopy(ref, ref, s_fwd.at[f, k], r_fwd.at[f, k], sibling)
+        ref = xe.at[f, 2 * k + core, pl.ds(80 * hf, 80)]
+        return rcopy(ref, ref, s_fwd.at[f, k, hf], r_fwd.at[f, k, hf], sibling)
 
     wz_start(0)
     wx_start(0, z)
     for f in range(2):
-        for dr in range(2):
-            row_copy(f, dr).start()
-        fwd_copy(f, 1, True).start()
-        wz_start(1 + f)
-    for n in (1, 2):
-        wx_start(n, z)
+        for hf in range(2):
+            for dr in range(2):
+                row_copy(f, dr, hf).start()
+        for hf in range(2):
+            fwd_copy(f, 1, hf, True).start()
+        if f == 0:
+            wz_start(1)
+            wx_start(1, z)
 
     def rows_forward(f):
-        for dr in range(2):
-            row_copy(f, dr).wait_recv()
-            fwd_copy(f, 2 * dr, True).start()
+        for hf in range(2):
+            for dr in range(2):
+                row_copy(f, dr, hf).wait_recv()
+                fwd_copy(f, 2 * dr, hf, True).start()
 
     def rows_wait(f):
         for k in range(3):
-            fwd_copy(f, k, False).wait_recv()
+            for hf in range(2):
+                fwd_copy(f, k, hf, False).wait_recv()
 
     weights_forward(0)
+    wz_start(2)
     weights_forward(1)
+    wx_start(2, z)
     rows_forward(0)
-    weights_forward(2)
     taps_in.wait()
 
     def gates_of(f):
@@ -223,17 +231,18 @@
         return (s * lax.rsqrt(jnp.sum(s * s, axis=-1, keepdims=True) + EPS)).astype(BF16)
 
     def step(i, carry):
-        f, slot = lax.div(i, 2), lax.rem(i, 2)
+        slot, f = lax.div(i, 2), lax.rem(i, 2)
 
         @pl.when(i == 1)
         def _():
-            weights_wait(1)
-
-        @pl.when(i == 2)
-        def _():
+            weights_forward(2)
             rows_forward(1)
             rows_wait(1)
             gates_of(1)
+
+        @pl.when(i == 2)
+        def _():
+            weights_wait(1)
 
         project(f, slot)
         head = 4 * par + 2 * c + slot
@@ -447,10 +456,11 @@
     for d in range(1, NX):
         px_copy(d, x).wait_send()
     for f in range(2):
-        for dr in range(2):
-            row_copy(f, dr).wait_send()
-        for k in range(3):
-            fwd_copy(f, k, True).wait_send()
+        for hf in range(2):
+            for dr in range(2):
+                row_copy(f, dr, hf).wait_send()
+            for k in range(3):
+                fwd_copy(f, k, hf, True).wait_send()
     pair.wait_send()
     for e in range(1, NZ):
 
@@ -496,7 +506,7 @@
             pltpu.VMEM((DK, DK), F32),
             pltpu.VMEM((DK, DK), BF16),
             pltpu.VMEM((2, NY, DK, DK), BF16),
-            sem((2, 2)), sem((2, 2)), sem((2, 3)), sem((2, 3)),
+            sem((2, 2, 2)), sem((2, 2, 2)), sem((2, 3, 2)), sem((2, 3, 2)),
             sem((3, 7)), sem((3, 7)), sem((3, 3, 8)), sem((3, 3, 8)),
             sem((2, 2)), sem((4,)), sem((2, 4)), sem((8,)), sem((2,)), sem((9,)),
             sem(()), sem(()), sem((3,)), sem((3,)),

time: 74 us -> 70.2 us (0.949)
  the two profiles are of different devices: /device:TPU:65 before, /device:TPU:193 now
where the time goes in v4:
time: 70.2 us; the launch traced here: 70 us
  Pallas kernels  68 us (97%)
  local copies, waits for them, and re-layouts  1.97 us (3%)
    pallas_call x1, Pallas kernels, mix(): pl.pallas_call(mix_kernel, out_shape=jax.ShapeDtypeStruct((2, 1, 160, 102...  68 us
    unnamed x1, local copies, waits for them, and re-layouts  1.97 us

profile of v4, /device:TPU:193, one launch (start us, length us, event | category | flops | bytes accessed | tf_op | source)
XLA Modules:
  0.0 70.0 jit_solution(10817824495544090318)
XLA Ops:
  0.0 68.0 %mix.1 = bf16[2,1,160,1024]{3,2,1,0:T(8,128)(2,1)} custom-call(bf16[2,160,1024]{2,1,0:T(8,128)(2,1)} %bitcast.3, bf16[32,3072]{1,0:T(8,128)(2,1)} %w_ref.1, bf16[8,1024]{1,0:T(8,128)(2,1)} %bitcast.4, f32[3,3,3072]{2,1,0:T(4,128)} %ck_hbm.1, f32[1,1024]{1,0:T(1,128)} %bitcast.5, f32[8]{0:T(128)} %rate_ref.1, f32[2,8]{1,0:T(2,128)} %decay_ref.1), custom_call_target="tpu_custom_call" | custom-call | tf_op jit(solution)/shard_map/mix/pallas_call | solution.py:485
  68.0 2.0 %copy.9 = bf16[2,1,160,1024]{3,2,1,0:T(8,128)(2,1)} copy(bf16[2,1,160,1024]{3,2,1,0:T(8,128)(2,1)} %mix.1) | data formatting | bytes 1310720

commit v5 on v4

--- a/solution.py
+++ b/solution.py
@@ -172,10 +172,10 @@
                 fwd_copy(f, k, hf, False).wait_recv()
 
     weights_forward(0)
+    weights_forward(1)
     wz_start(2)
-    weights_forward(1)
+    rows_forward(0)
     wx_start(2, z)
-    rows_forward(0)
     taps_in.wait()
 
     def gates_of(f):
@@ -231,18 +231,18 @@
         return (s * lax.rsqrt(jnp.sum(s * s, axis=-1, keepdims=True) + EPS)).astype(BF16)
 
     def step(i, carry):
-        slot, f = lax.div(i, 2), lax.rem(i, 2)
+        f, slot = lax.div(i, 2), lax.rem(i, 2)
 
         @pl.when(i == 1)
         def _():
             weights_forward(2)
             rows_forward(1)
+            weights_wait(1)
+
+        @pl.when(i == 2)
+        def _():
             rows_wait(1)
             gates_of(1)
-
-        @pl.when(i == 2)
-        def _():
-            weights_wait(1)
 
         project(f, slot)
         head = 4 * par + 2 * c + slot
@@ -356,7 +356,7 @@
         core = c if sending else 1 - c
         return rcopy(zin.at[core, k], zin.at[core, k], s_zs.at[k], r_zs.at[k], sibling)
 
-    for e in range(NZ - 1, 0, -1):
+    for e in range(1, NZ):
 
         @pl.when(z + e < NZ)
         def _():

time: 70.2 us -> 68.3 us (0.973)
  the two profiles are of different devices: /device:TPU:193 before, /device:TPU:385 now
where the time goes in v5:
time: 68.3 us; the launch traced here: 68.1 us
  Pallas kernels  66.1 us (97%)
  local copies, waits for them, and re-layouts  1.97 us (3%)
    pallas_call x1, Pallas kernels, mix(): pl.pallas_call(mix_kernel, out_shape=jax.ShapeDtypeStruct((2, 1, 160, 102...  66.1 us
    unnamed x1, local copies, waits for them, and re-layouts  1.97 us

profile of v5, /device:TPU:385, one launch (start us, length us, event | category | flops | bytes accessed | tf_op | source)
XLA Modules:
  0.0 68.1 jit_solution(13973368613208682661)
XLA Ops:
  0.0 66.1 %mix.1 = bf16[2,1,160,1024]{3,2,1,0:T(8,128)(2,1)} custom-call(bf16[2,160,1024]{2,1,0:T(8,128)(2,1)} %bitcast.3, bf16[32,3072]{1,0:T(8,128)(2,1)} %w_ref.1, bf16[8,1024]{1,0:T(8,128)(2,1)} %bitcast.4, f32[3,3,3072]{2,1,0:T(4,128)} %ck_hbm.1, f32[1,1024]{1,0:T(1,128)} %bitcast.5, f32[8]{0:T(128)} %rate_ref.1, f32[2,8]{1,0:T(2,128)} %decay_ref.1), custom_call_target="tpu_custom_call" | custom-call | tf_op jit(solution)/shard_map/mix/pallas_call | solution.py:485
  66.1 2.0 %copy.9 = bf16[2,1,160,1024]{3,2,1,0:T(8,128)(2,1)} copy(bf16[2,1,160,1024]{3,2,1,0:T(8,128)(2,1)} %mix.1) | data formatting | bytes 1310720

commit v6 on v5

--- a/solution.py
+++ b/solution.py
@@ -60,14 +60,14 @@
     ) + jnp.dot(a_high, b_low, preferred_element_type=F32)
 
 
-def inverse(system, ident):
+def solve(system, ident, right):
     power = ident - 0.4 * system
-    total = ident + power
-    power = close(power, power)
-    for _ in range(3):
-        stacked = close(jnp.concatenate([power, total], axis=0), power)
-        power, total = stacked[:DK], total + stacked[DK:]
-    return 0.4 * (total + close(total, power))
+    sums = jnp.concatenate([ident, right], axis=1)
+    for k in range(5):
+        moved = close(power, jnp.concatenate([power, sums], axis=1) if k < 4 else sums)
+        sums = sums + (moved[:, DK:] if k < 4 else moved)
+        power = moved[:, :DK]
+    return 0.4 * sums
 
 
 def mix_kernel(
@@ -207,6 +207,7 @@
                 xe[f].reshape(960, 1024), wg[n].reshape(1024, 256), preferred_element_type=F32
             )
             .astype(BF16)
+            .astype(F32)
             .reshape(6, 160, 256)
         )
 
@@ -215,7 +216,7 @@
         scale = {(0, 2): low, (1, 0): low, (2, 2): high, (3, 0): high}
         sums = [None] * 3
         for a in range(3):
-            row = proj[o + a, :, half * 128 : (half + 1) * 128].astype(F32)
+            row = proj[o + a, :, half * 128 : (half + 1) * 128]
             for b in range(3):
                 tap = ck_ref[a, pl.ds(b, 1), pl.ds(col, 128)]
                 tap = tap * scale[(o, a)] if (o, a) in scale else tap
@@ -322,9 +323,9 @@
         jnp.int32, (DK, DK), 1
     )
     ident = jnp.where(diagonal, 1.0, 0.0)
-    solved = inverse(ident + (0.5 * step_size) * (gram + gram.T), ident)
-    own[:, :DK] = (retain * solved).astype(BF16)
-    own[:, DK:] = (retain * close(solved, step_size * written)).astype(BF16)
+    maps = solve(ident + (0.5 * step_size) * (gram + gram.T), ident, step_size * written)
+    own[:, :DK] = (retain * maps[:, :DK]).astype(BF16)
+    own[:, DK:] = (retain * maps[:, DK:]).astype(BF16)
 
     def compose(latter, earlier):
         both = jnp.dot(latter[:, :DK], earlier, preferred_element_type=F32)
@@ -491,7 +492,7 @@
             pltpu.VMEM((2, 6, 160, 1024), BF16),
             pltpu.VMEM((3, NZ, NX, 32, 256), BF16),
             pltpu.VMEM((3, 3, 3072), F32),
-            pltpu.VMEM((6, 160, 256), BF16),
+            pltpu.VMEM((6, 160, 256), F32),
             pltpu.VMEM((640, 256), BF16),
             pltpu.VMEM((640, DK), BF16),
             pltpu.VMEM((2, 2, 640, DK), F32),

time: 68.3 us -> 68.2 us (level)
  no operation moved by 1% of the time
where the time goes in v6:
time: 68.2 us; the launch traced here: 67.9 us
  Pallas kernels  66 us (97%)
  local copies, waits for them, and re-layouts  1.97 us (3%)
    pallas_call x1, Pallas kernels, mix(): pl.pallas_call(mix_kernel, out_shape=jax.ShapeDtypeStruct((2, 1, 160, 102...  66 us
    unnamed x1, local copies, waits for them, and re-layouts  1.97 us

profile of v6, /device:TPU:385, one launch (start us, length us, event | category | flops | bytes accessed | tf_op | source)
XLA Modules:
  0.0 67.9 jit_solution(13913729370909925976)
XLA Ops:
  0.0 66.0 %mix.1 = bf16[2,1,160,1024]{3,2,1,0:T(8,128)(2,1)} custom-call(bf16[2,160,1024]{2,1,0:T(8,128)(2,1)} %bitcast.3, bf16[32,3072]{1,0:T(8,128)(2,1)} %w_ref.1, bf16[8,1024]{1,0:T(8,128)(2,1)} %bitcast.4, f32[3,3,3072]{2,1,0:T(4,128)} %ck_hbm.1, f32[1,1024]{1,0:T(1,128)} %bitcast.5, f32[8]{0:T(128)} %rate_ref.1, f32[2,8]{1,0:T(2,128)} %decay_ref.1), custom_call_target="tpu_custom_call" | custom-call | tf_op jit(solution)/shard_map/mix/pallas_call | solution.py:486
  66.0 2.0 %copy.9 = bf16[2,1,160,1024]{3,2,1,0:T(8,128)(2,1)} copy(bf16[2,1,160,1024]{3,2,1,0:T(8,128)(2,1)} %mix.1) | data formatting | bytes 1310720
